TPU v7x, 1024 devices: a whole 8x8x8 slice. The times are simulated.
1024 devices in a mesh: fsdp: 64 (over z, y), tp: 16 (over x, core).
Axes of the slice: x: 8, y: 8, z: 8, core: 2. Of those that a mesh axis runs over, the one named last changes fastest.
Arguments:
- momentum: float32 [8192, 28672], P('tp', 'fsdp'), may hold values from -16 to 16
- gradient: bfloat16 [8192, 28672], P('tp', 'fsdp'), may hold values from -40 to 40
- factor: float32 [28672, 512], P('fsdp'), may hold values from -6 to 6
Outputs:
- momentum_new: float32 [8192, 28672], P('tp', 'fsdp')
- factor_new: float32 [28672, 512], P('fsdp')
- update: bfloat16 [8192, 28672], P('tp', 'fsdp')
All inputs are finite; a program needn't handle non-finite values.
Results may differ from a plain program's by a relative error of at most 0.005.
The roundings to bfloat16 on the way count: a program that leaves them out, or rounds other values in their place, can miss the bound.
Values may be sent and summed in bfloat16 or wider, within the bound.
No kernel may reach another device: no remote copies, remote signals or barrier semaphores. Data moves between devices by JAX's collectives and lax.ppermute only.
A program may use at most 32 MiB of HBM per device.

v0:
```python
import math

import jax
import jax.numpy as jnp
from jax import lax
from jax.sharding import PartitionSpec as P

D = 8192
FF = 28672
RANK = 512


feedback = 0.05
epsilon = 1e-06


def orthonormal(left_rows, gram_sum):
    chol_lower = jnp.linalg.cholesky(gram_sum)
    solved = lax.linalg.triangular_solve(
        chol_lower, left_rows, left_side=False, lower=True, transpose_a=True
    )
    return solved.astype(jnp.bfloat16)


def gram_of(left_rows):
    return lax.dot_general(
        left_rows,
        left_rows,
        (((0,), (0,)), ((), ())),
        precision=lax.Precision.HIGHEST,
        preferred_element_type=jnp.float32,
    )


def per_device(momentum, gradient, factor):
    blended = momentum + gradient.astype(jnp.float32)
    blend_low = blended.astype(jnp.bfloat16)
    factor_low = factor.astype(jnp.bfloat16)
    left_share = lax.psum_scatter(
        jnp.dot(blend_low, factor_low, preferred_element_type=jnp.float32),
        "fsdp",
        scatter_dimension=0,
        tiled=True,
    )
    gram_sum = lax.psum(gram_of(left_share), ("fsdp", "tp"))
    ortho_share = orthonormal(left_share, gram_sum)
    left_low = lax.all_gather(ortho_share, "fsdp", axis=0, tiled=True)
    right_term = lax.dot_general(
        blend_low, left_low, (((0,), (0,)), ((), ())), preferred_element_type=jnp.float32
    )
    right_full = lax.psum(right_term, "tp")
    squares = lax.psum(jnp.sum(right_full * right_full, axis=0), "fsdp")
    col_scale = jnp.sqrt(squares / FF + epsilon)
    factor_new = right_full / col_scale[None, :]
    feed_term = lax.dot_general(
        left_low,
        right_full.astype(jnp.bfloat16),
        (((1,), (1,)), ((), ())),
        preferred_element_type=jnp.float32,
    )
    momentum_new = blended - feedback * feed_term
    update_full = lax.dot_general(
        left_low,
        factor_new.astype(jnp.bfloat16),
        (((1,), (1,)), ((), ())),
        preferred_element_type=jnp.float32,
    )
    update = (math.sqrt(D / RANK) * update_full).astype(jnp.bfloat16)
    return (momentum_new, factor_new, update)


def solution(mesh):
    return jax.shard_map(
        per_device,
        mesh=mesh,
        in_specs=(P("tp", "fsdp"), P("tp", "fsdp"), P("fsdp", None)),
        out_specs=(P("tp", "fsdp"), P("fsdp", None), P("tp", "fsdp")),
        check_vma=False,
    )
```

profile of v0, /device:TPU:8, one launch (start us, length us, event | category | flops | bytes accessed | tf_op | source)
XLA Modules:
  0.0 947.5 jit_solution(11081743158971510155)
XLA Ops:
  7.2 3.1 fusion.6
  10.4 1.3 dynamic-slice.3
  12.3 184.5 %all-reduce.10.cloned.1.call-done = f32[512,512]{1,0:T(8,128)} async-done(((f32[512,512]{1,0:T(8,128)}), f32[512,512]{1,0:T(8,128)}) %all-reduce.10.cloned.1.call-update) | async-done | bytes 1048592
  196.8 2.8 fusion.25
  199.7 287.4 %all-reduce.6.cloned.1.call-done = f32[512,512]{0,1:T(8,128)} async-done(((f32[512,512]{0,1:T(8,128)}), f32[512,512]{0,1:T(8,128)}) %all-reduce.6.cloned.1.call-update) | async-done | bytes 1048592 | tf_op jit(solution)/shard_map/psum | solution.py:45
  487.1 1.6 copy.9
  489.0 11.7 %cholesky.104 = f32[128,128]{1,0:T(8,128)S(1)} custom-call(f32[128,128]{1,0:T(8,128)S(1)} %cholesky.266), custom_call_target="Cholesky" | custom-call | tf_op jit(solution)/shard_map/jit(cholesky)/cholesky | solution.py:18
  500.8 9.8 %custom-call.30 = f32[1,128,128]{1,2,0:T(8,128)S(1)} custom-call(f32[1,128,128]{2,1,0:T(8,128)S(1)} %get-tuple-element.30), custom_call_target="InvertDiagBlocksLowerTriangular" | custom-call | tf_op jit(solution)/shard_map/jit(cholesky)/cholesky | solution.py:18
  511.4 11.7 %cholesky.217 = f32[128,128]{1,0:T(8,128)S(1)} custom-call(f32[128,128]{1,0:T(8,128)S(1)} %cholesky.270), custom_call_target="Cholesky" | custom-call | tf_op jit(solution)/shard_map/jit(cholesky)/cholesky | solution.py:18
  523.1 10.0 %custom-call.31 = f32[1,128,128]{1,2,0:T(8,128)S(1)} custom-call(f32[1,128,128]{2,1,0:T(8,128)S(1)} %get-tuple-element.27), custom_call_target="InvertDiagBlocksLowerTriangular" | custom-call | tf_op jit(solution)/shard_map/jit(cholesky)/cholesky | solution.py:18
  533.8 11.7 %cholesky.238 = f32[128,128]{1,0:T(8,128)S(1)} custom-call(f32[128,128]{1,0:T(8,128)S(1)} %cholesky.275), custom_call_target="Cholesky" | custom-call | tf_op jit(solution)/shard_map/jit(cholesky)/cholesky | solution.py:18
  545.5 0.7 compare_reduce_fusion.1
  546.2 9.8 %custom-call.32 = f32[1,128,128]{1,2,0:T(8,128)S(1)} custom-call(f32[1,128,128]{2,1,0:T(8,128)S(1)} %get-tuple-element.24), custom_call_target="InvertDiagBlocksLowerTriangular" | custom-call | tf_op jit(solution)/shard_map/jit(cholesky)/cholesky | solution.py:18
  556.6 11.7 %cholesky.255 = f32[128,128]{1,0:T(8,128)S(1)} custom-call(f32[128,128]{1,0:T(8,128)S(1)} %convolution_subtract_fusion.2), custom_call_target="Cholesky" | custom-call | tf_op jit(solution)/shard_map/jit(cholesky)/cholesky | solution.py:18
  568.4 0.6 compare_reduce_fusion
  572.6 8.0 while.1
  573.2 1.4 bitcast_dynamic-update-slice_fusion.2
  575.2 1.4 bitcast_dynamic-update-slice_fusion.2
  577.2 1.4 bitcast_dynamic-update-slice_fusion.2
  579.2 1.4 bitcast_dynamic-update-slice_fusion.2
  580.6 39.3 %custom-call.33 = f32[4,128,128]{1,2,0:T(8,128)S(1)} custom-call(f32[4,128,128]{2,1,0:T(8,128)S(1)} %get-tuple-element.10), custom_call_target="InvertDiagBlocksLowerTriangular" | custom-call | tf_op jit(solution)/shard_map/triangular_solve | solution.py:19
  619.9 0.8 fusion.46
  620.8 0.9 convolution_subtract_fusion.5
  621.9 0.9 convolution_subtract_fusion.4
  623.0 1.0 convolution_subtract_fusion.3
  624.1 48.6 %all_gather.3 = bf16[512,512]{1,0:T(8,128)(2,1)S(1)} all-gather(bf16[8,512]{1,0:T(8,128)(2,1)S(1)} %pad_maximum_fusion), channel_id=1, replica_groups=mesh['fsdp'=64,'tp'=16] {'fsdp'}, dimensions={0}, use_global_device_ids=true | all-gather | bytes 532480 | tf_op jit(solution)/shard_map/all_gather | solution.py:47
  672.7 1.3 fusion.40
  674.1 117.2 %all-reduce.8.cloned.1.call-done = f32[448,512]{1,0:T(8,128)} async-done(((f32[448,512]{1,0:T(8,128)}), f32[448,512]{1,0:T(8,128)}) %all-reduce.8.cloned.1.call-update) | async-done | bytes 917520 | tf_op jit(solution)/shard_map/psum | solution.py:51
  791.3 1.4 multiply_reduce_fusion
  792.6 145.6 %psum.23 = f32[512]{0:T(512)S(1)} all-reduce(f32[512]{0:T(512)S(1)} %multiply_reduce_fusion), channel_id=1, replica_groups=mesh['fsdp'=64,'tp'=16] {'fsdp'}, use_global_device_ids=true, to_apply=%region_12.13 | all-reduce | flops 512 | bytes 4096 | tf_op jit(solution)/shard_map/psum | solution.py:52
  938.4 1.2 fusion.1
  939.6 1.4 fusion
  (50 shorter events, 6.7 us)
Async XLA Ops:
  7.2 189.6 %all-reduce.10.cloned.1.call-start = ((), (), s32[]{:S(2)}) async-start(), calls=%async_computation.2 | async-start | bytes 2097152
  10.4 476.7 %all-reduce.6.cloned.1.call-start = ((), (), s32[]{:S(2)}) async-start(), calls=%async_computation | async-start | bytes 2097152 | tf_op jit(solution)/shard_map/psum | solution.py:45
  199.6 591.6 %all-reduce.8.cloned.1.call-start = ((), (), s32[]{:S(2)}) async-start(), calls=%async_computation.1 | async-start | bytes 1835008 | tf_op jit(solution)/shard_map/psum | solution.py:51
  487.1 1.7 copy-start.2
  572.6 100.1 %copy-start = (f32[512,448]{0,1:T(8,128)S(1)}, f32[512,448]{0,1:T(8,128)}, u32[]{:S(2)}) copy-start(f32[512,448]{0,1:T(8,128)} %param.3) | copy-start | bytes 2752516
  622.8 49.9 %copy-start.3 = (bf16[512,448]{0,1:T(8,128)(2,1)S(1)}, bf16[512,448]{0,1:T(8,128)(2,1)}, u32[]{:S(2)}) copy-start(bf16[512,448]{0,1:T(8,128)(2,1)} %param.4) | copy-start | bytes 1376260
  791.3 147.0 %copy-start.1 = (f32[448,512]{1,0:T(8,128)S(1)}, f32[448,512]{1,0:T(8,128)}, u32[]{:S(2)}) copy-start(f32[448,512]{1,0:T(8,128)} %all-reduce.8.cloned.1.call-done) | copy-start | bytes 2752516
  938.4 1.2 copy-start.4
Sparse Core Ops, SparseCore 0:
  11.2 185.5 all-reduce.9
  202.3 284.7 all-reduce.5
  674.2 117.0 all-reduce.7
where the time goes:
time: 948 us
  waiting for transfers between devices  589 us (62%)
  blocking collectives  194 us (20%)
  other arithmetic  120 us (13%)
  between operations  17.2 us (2%)
  matrix products  15.9 us (2%)
  local copies, waits for them, and re-layouts  11 us (1%)
    psum x1, waiting for transfers between devices, per_device(): gram_sum = lax.psum(gram_of(left_share), ('fsdp', 'tp'))  287 us
    unnamed x4, waiting for transfers between devices  185 us
    psum x1, blocking collectives, per_device(): squares = lax.psum(jnp.sum(right_full * right_full, axis=0), 'fsdp')  146 us
    psum x1, waiting for transfers between devices, per_device(): right_full = lax.psum(right_term, 'tp')  117 us
    another operation x14, other arithmetic, orthonormal(): chol_lower = jnp.linalg.cholesky(gram_sum)  78.6 us
    all_gather x1, blocking collectives, per_device(): left_low = lax.all_gather(ortho_share, 'fsdp', axis=0, tiled=True)  48.6 us
    another operation x4, other arithmetic, orthonormal(): lax.linalg.triangular_solve(chol_lower, left_rows, left_side=False, lower...  39.7 us
  transfers between devices with their start and end apart: 3, of which 3 were waited for; matrix products, arithmetic and copies ran while one was open for 0% of the time, Pallas kernels for 0%

commit v1 on v0

v1 whole, which is shorter than its diff:
```python
import functools
import math

import jax
import jax.numpy as jnp
from jax import lax
from jax.experimental import pallas as pl
from jax.experimental.pallas import tpu as pltpu
from jax.sharding import Mesh, PartitionSpec as P

D = 8192
FF = 28672
RANK = 512
NB = 128
HALF = RANK // 2

feedback = 0.05
epsilon = 1e-06

ZY = ("z", "y")
EXACT = lax.Precision.HIGHEST
VMEM = pl.BlockSpec(memory_space=pltpu.VMEM)
SMEM = pl.BlockSpec(memory_space=pltpu.SMEM)
f32 = jnp.float32
bf16 = jnp.bfloat16


def dot(a, b, contract, precision=None):
    return lax.dot_general(
        a, b, (contract, ((), ())), precision=precision, preferred_element_type=f32
    )


def call(kernel, outs, *args, scratch=()):
    specs = [SMEM if a.dtype == jnp.int32 else VMEM for a in args]
    return pl.pallas_call(
        kernel,
        out_shape=outs,
        in_specs=specs,
        out_specs=jax.tree.map(lambda _: VMEM, outs),
        scratch_shapes=scratch,
        compiler_params=pltpu.CompilerParams(vmem_limit_bytes=40 * 2**20),
    )(*args)


def shape(dims, dtype):
    return jax.ShapeDtypeStruct(dims, dtype)


def gram_kernel(where_ref, left_ref, keep_ref, send_ref):
    left = left_ref[...]
    first = where_ref[0] * 8
    row = lax.broadcasted_iota(jnp.int32, (RANK, 8), 0)
    col = lax.broadcasted_iota(jnp.int32, (RANK, 8), 1)
    pick = jnp.where(row == first + col, 1.0, 0.0)
    columns = dot(left, pick, ((1,), (0,)), EXACT)
    rows = dot(columns, left, ((0,), (0,)), EXACT)
    own_low = where_ref[1] == 0
    low, high = rows[:, :HALF], rows[:, HALF:]
    keep_ref[...] = jnp.where(own_low, low, high)
    send_ref[...] = jnp.where(own_low, high, low)


def row_of(x, k):
    return jnp.broadcast_to(x[k : k + 1, :], (8, NB))


def lane_of(x, c):
    return jnp.broadcast_to(x[:, c : c + 1], (8, NB))


def diag_inverse(d):
    sub = lax.broadcasted_iota(jnp.int32, (8, NB), 0)
    lane = lax.broadcasted_iota(jnp.int32, (8, NB), 1)
    d = list(d)
    e = [jnp.where(lane == sub + 8 * i, 1.0, 0.0) for i in range(16)]
    out = []
    for t in range(16):
        s, g, f = d[t], e[t], e[t]
        cols = [lane_of(s, 8 * t + k) for k in range(8)]
        pivots = jnp.zeros((8, NB), f32)
        for k in range(8):
            own = sub == k
            pivot = row_of(cols[k], k)
            inv = 1.0 / pivot
            pivots = jnp.where(own, pivot, pivots)
            col = cols[k]
            for c in range(k + 1, 8):
                r = row_of(cols[c], k) * inv
                cols[c] = jnp.where(own, r, cols[c] - col * r)
            f = jnp.where(sub > k, f - col * (row_of(f, k) * inv), f)
            if t < 15:
                r = row_of(s, k) * inv
                s = jnp.where(own, r, s - col * r)
                r = row_of(g, k) * inv
                g = jnp.where(own, r, g - col * r)
        out.append(f * lax.rsqrt(pivots))
        for i in range(t + 1, 16):
            di, ei = d[i], e[i]
            u = [lane_of(d[i], 8 * t + k) for k in range(8)]
            for k in range(8):
                di = di - u[k] * row_of(s, k)
                ei = ei - u[k] * row_of(g, k)
            d[i], e[i] = di, ei
    return out


def ortho_kernel(
    where_ref, own_ref, other_ref, left_ref, mom_ref, grad_ref,
    q_ref, keep_ref, send_ref, a_ref, l_ref, w_ref,
):
    core = where_ref[1]
    a_ref[:, pl.ds(pl.multiple_of(core * HALF, HALF), HALF)] = own_ref[...]
    a_ref[:, pl.ds(pl.multiple_of((1 - core) * HALF, HALF), HALF)] = other_ref[...]
    l_ref[...] = left_ref[...]

    def outer(j, carry):
        j0 = pl.multiple_of(j * NB, NB)
        tiles = [
            a_ref[pl.ds(pl.multiple_of(j0 + 8 * i, 8), 8), pl.ds(j0, NB)]
            for i in range(16)
        ]
        for i, tile in enumerate(diag_inverse(tiles)):
            w_ref[8 * i : 8 * i + 8, :] = tile
        w = w_ref[...]
        panel = dot(w, a_ref[pl.ds(j0, NB), :], ((1,), (0,)), EXACT)
        lane = lax.broadcasted_iota(jnp.int32, (NB, RANK), 1)
        panel = jnp.where(lane >= j0 + NB, panel, 0.0)
        q = dot(l_ref[:, pl.ds(j0, NB)], w, ((1,), (1,)), EXACT)
        q_ref[:, pl.ds(j0, NB)] = q.astype(bf16)
        a_ref[...] -= dot(panel, panel, ((0,), (0,)), EXACT)
        l_ref[...] -= dot(q, panel, ((1,), (0,)), EXACT)
        return carry

    lax.fori_loop(0, RANK // NB, outer, 0)
    blend_low = (mom_ref[...] + grad_ref[...].astype(f32)).astype(bf16)
    right = dot(blend_low, q_ref[...], ((1,), (0,)))
    low, high = right[:, :HALF], right[:, HALF:]
    keep_ref[...] = jnp.where(core == 0, low, high)
    send_ref[...] = jnp.where(core == 0, high, low)


def whole(core, own_ref, other_ref):
    own, other = own_ref[...], other_ref[...]
    first = jnp.where(core == 0, own, other)
    second = jnp.where(core == 0, other, own)
    return jnp.concatenate([first, second], axis=1)


def momentum_kernel(where_ref, own_ref, other_ref, q_ref, mom_ref, grad_ref, out_ref, squares_ref):
    right = whole(where_ref[1], own_ref, other_ref)
    feed = dot(right, q_ref[...], ((1,), (1,)))
    out_ref[...] = mom_ref[...] + grad_ref[...].astype(f32) - feedback * feed
    wide = right.astype(f32)
    squares_ref[...] = jnp.sum(wide * wide, axis=0, keepdims=True)


def update_kernel(where_ref, own_ref, other_ref, q_ref, squares_ref, factor_ref, update_ref):
    right = whole(where_ref[1], own_ref, other_ref).astype(f32)
    mean = jnp.sum(squares_ref[...], axis=0, keepdims=True) / FF
    factor_new = right / jnp.sqrt(mean + epsilon)
    factor_ref[...] = factor_new
    update = dot(factor_new.astype(bf16), q_ref[...], ((1,), (1,)))
    update_ref[...] = (math.sqrt(D / RANK) * update).astype(bf16)


def to_all(x, axes, n):
    return lax.all_to_all(jnp.broadcast_to(x[None], (n,) + x.shape), axes, 0, 0)


def swap(x):
    return lax.ppermute(x, "core", [(0, 1), (1, 0)])


def per_device(nz, ny, nx, momentum, gradient, factor):
    n = nz * ny
    rows = momentum.shape[0] // n
    width = momentum.shape[1]
    blended = momentum + gradient.astype(f32)
    left_part = jnp.dot(
        blended.astype(bf16), factor.astype(bf16), preferred_element_type=f32
    )
    where = jnp.stack([lax.axis_index(ZY), lax.axis_index("core")]).astype(jnp.int32)
    mom_t, grad_t = momentum.T, gradient.T

    pieces = lax.all_to_all(left_part.reshape(n, rows, RANK), ZY, 0, 0)
    left = to_all(jnp.sum(pieces, axis=0), ZY, n).reshape(n * rows, RANK)

    keep, send = call(gram_kernel, (shape((8, HALF), f32),) * 2, where, left)
    gram_rows = jnp.sum(to_all(keep + swap(send), "x", nx), axis=0)
    gram_own = to_all(gram_rows, ZY, n).reshape(RANK, HALF)
    gram_other = swap(gram_own)

    left_low, keep, send = call(
        ortho_kernel,
        (shape(left.shape, bf16),) + (shape((width, HALF), f32),) * 2,
        where, gram_own, gram_other, left, mom_t, grad_t,
        scratch=[
            pltpu.VMEM((RANK, RANK), f32),
            pltpu.VMEM(left.shape, f32),
            pltpu.VMEM((NB, NB), f32),
        ],
    )
    part = (keep + swap(send)).reshape(nx, width // nx, HALF)
    mine = jnp.sum(lax.all_to_all(part, "x", 0, 0), axis=0).astype(bf16)
    own = to_all(mine, "x", nx).reshape(width, HALF)
    other = swap(own)

    momentum_t, squares = call(
        momentum_kernel,
        (shape((width, left.shape[0]), f32), shape((1, RANK), f32)),
        where, own, other, left_low, mom_t, grad_t,
    )
    squares = to_all(squares, ZY, n).reshape(n, RANK)
    factor_new, update_t = call(
        update_kernel,
        (shape((width, RANK), f32), shape((width, left.shape[0]), bf16)),
        where, own, other, left_low, squares,
    )
    return (momentum_t.T, factor_new, update_t.T)


def solution(mesh):
    nz = ny = math.isqrt(mesh.shape["fsdp"])
    nx = mesh.shape["tp"] // 2
    grid = Mesh(mesh.devices.reshape(nz, ny, nx, 2), ("z", "y", "x", "core"))
    tp = ("x", "core")
    return jax.shard_map(
        functools.partial(per_device, nz, ny, nx),
        mesh=grid,
        in_specs=(P(tp, ZY), P(tp, ZY), P(ZY, None)),
        out_specs=(P(tp, ZY), P(ZY, None), P(tp, ZY)),
        check_vma=False,
    )
```

time: 948 us -> 233 us (0.25)
  the two profiles are of different devices: /device:TPU:8 before, /device:TPU:1 now
where the time goes in v1:
time: 233 us; the launch traced here: 232 us
  blocking collectives  135 us (58%)
  Pallas kernels  35.6 us (15%)
  waiting for transfers between devices  30.7 us (13%)
  starting transfers between devices  26.7 us (11%)
    all_to_all x4, blocking collectives, to_all(): return lax.all_to_all(jnp.broadcast_to(x[None], (n,) + x.shape), axes, 0, 0)  64.7 us
    all_to_all x1, blocking collectives, per_device(): pieces = lax.all_to_all(left_part.reshape(n, rows, RANK), ZY, 0, 0)  51.2 us
    pallas_call x4, Pallas kernels, call(): pl.pallas_call(kernel, out_shape=outs, in_specs=specs, out_specs=jax.tree...  35.6 us
    all_to_all x1, waiting for transfers between devices, to_all(): return lax.all_to_all(jnp.broadcast_to(x[None], (n,) + x.shape), axes, 0, 0)  25.8 us
    all_to_all x1, blocking collectives, per_device(): mine = jnp.sum(lax.all_to_all(part, 'x', 0, 0), axis=0).astype(bf16)  19 us
    ppermute x4, starting transfers between devices, swap(): return lax.ppermute(x, 'core', [(0, 1), (1, 0)])  19 us
    all_to_all x1, starting transfers between devices, to_all(): return lax.all_to_all(jnp.broadcast_to(x[None], (n,) + x.shape), axes, 0, 0)  7.72 us
    ppermute x4, waiting for transfers between devices, swap(): return lax.ppermute(x, 'core', [(0, 1), (1, 0)])  4.84 us
  transfers between devices with their start and end apart: 5, of which 5 were waited for; matrix products, arithmetic and copies ran while one was open for 0% of the time, Pallas kernels for 0%

profile of v1, /device:TPU:1, one launch (start us, length us, event | category | flops | bytes accessed | tf_op | source)
XLA Modules:
  0.0 232.2 jit_solution(12616083056778725115)
XLA Ops:
  0.6 2.1 convolution_bitcast_fusion
  2.7 51.2 %all_to_all.35 = f32[64,8,512]{2,1,0:T(8,128)S(1)} all-to-all(f32[64,8,512]{2,1,0:T(8,128)S(1)} %convolution_bitcast_fusion), channel_id=1, replica_groups=mesh['z'=8,'y'=8,'x'=8,'core'=2] {'z','y'}, dimensions={0} | all-to-all | bytes 2097152 | tf_op jit(solution)/shard_map/all_to_all | solution.py:186
  53.9 0.1 reduce_sum.27
  54.0 1.1 broadcast_in_dim.12
  55.1 7.7 %all-to-all-start.1 = ((f32[64,8,512]{2,1,0:T(8,128)}), f32[64,8,512]{2,1,0:T(8,128)S(1)}, u32[]{:S(2)}, u32[]{:S(2)}) async-start(f32[64,8,512]{2,1,0:T(8,128)} %broadcast_in_dim.12), calls=%async_computation.1 | async-start | bytes 2097152 | tf_op jit(solution)/shard_map/all_to_all | solution.py:168
  62.8 0.1 pad_add_fusion.where_ref
  62.9 25.8 %all-to-all-done.1 = f32[64,8,512]{2,1,0:T(8,128)S(1)} async-done(((f32[64,8,512]{2,1,0:T(8,128)}), f32[64,8,512]{2,1,0:T(8,128)S(1)}, u32[]{:S(2)}, u32[]{:S(2)}) %all-to-all-start.1) | async-done | bytes 1048608 | tf_op jit(solution)/shard_map/all_to_all | solution.py:168
  88.8 2.8 %shard_map.58 = (f32[8,256]{1,0:T(8,128)S(1)}, f32[8,256]{1,0:T(8,128)S(1)}) custom-call(s32[2]{0:T(128)S(1)} %pad_add_fusion.where_ref, f32[512,512]{1,0:T(8,128)S(1)} %bitcast.16), custom_call_target="tpu_custom_call" | custom-call | tf_op jit(solution)/shard_map/pallas_call | solution.py:36
  91.5 6.7 %collective-permute-start = (f32[8,256]{1,0:T(8,128)S(1)}, f32[8,256]{1,0:T(8,128)S(1)}, u32[]{:S(2)}, u32[]{:S(2)}) collective-permute-start(f32[8,256]{1,0:T(8,128)S(1)} %get-tuple-element.13), channel_id=1, source_target_pairs={{0,1},{1,0},{2,3},{3,2},{4,5},{5,4},{6,7},{7,6},{8,9},{9,8},{10,11... | collective-permute-start | bytes 24584 | tf_op jit(solution)/shard_map/ppermute | solution.py:172
  98.3 0.8 collective-permute-done
  99.1 0.0 copy-start
  99.1 13.7 %all_to_all.36 = f32[8,8,256]{2,1,0:T(8,128)S(1)} all-to-all(f32[8,8,256]{2,1,0:T(8,128)S(1)} %broadcast_in_dim.13), channel_id=1, replica_groups=mesh['z'=8,'y'=8,'x'=8,'core'=2] {'x'}, dimensions={0} | all-to-all | bytes 131072 | tf_op jit(solution)/shard_map/all_to_all | solution.py:168
  112.8 0.0 copy-start.1
  112.8 21.6 %all_to_all.37 = f32[64,8,256]{2,1,0:T(8,128)S(1)} all-to-all(f32[64,8,256]{2,1,0:T(8,128)S(1)} %broadcast_in_dim.14), channel_id=1, replica_groups=mesh['z'=8,'y'=8,'x'=8,'core'=2] {'z','y'}, dimensions={0} | all-to-all | bytes 1048576 | tf_op jit(solution)/shard_map/all_to_all | solution.py:168
  134.4 7.0 %collective-permute-start.1 = (f32[512,256]{1,0:T(8,128)S(1)}, f32[512,256]{1,0:T(8,128)S(1)}, u32[]{:S(2)}, u32[]{:S(2)}) collective-permute-start(f32[512,256]{1,0:T(8,128)S(1)} %bitcast.22), channel_id=1, source_target_pairs={{0,1},{1,0},{2,3},{3,2},{4,5},{5,4},{6,7},{7,6},{8,9},{9,8},{10,11... | collective-permute-start | bytes 1572872 | tf_op jit(solution)/shard_map/ppermute | solution.py:172
  141.4 1.5 collective-permute-done.1.other_ref
  142.9 0.0 copy-done
  142.9 0.0 copy-done.1
  142.9 29.0 %shard_map.59 = (bf16[512,512]{1,0:T(8,128)(2,1)S(1)}, f32[448,256]{1,0:T(8,128)S(1)}, f32[448,256]{1,0:T(8,128)S(1)}) custom-call(s32[2]{0:T(128)S(1)} %pad_add_fusion.where_ref, f32[512,256]{1,0:T(8,128)S(1)} %bitcast.23, f32[512,256]{1,0:T(8,128)S(1)} %collective-permute-done.1.other_ref, f32[512,512]{1,0:T(8,128)S(1)} %bitcast.17, ...), custom_call_target="tpu_custom_call" | custom-call | tf_op jit(solution)/shard_map/pallas_call | solution.py:36
  172.0 2.3 collective-permute-start.2
  174.2 1.4 collective-permute-done.2
  175.7 0.1 add.15
  175.7 19.0 %all_to_all.38 = f32[8,56,256]{2,1,0:T(8,128)S(1)} all-to-all(f32[8,56,256]{2,1,0:T(8,128)S(1)} %bitcast.29), channel_id=1, replica_groups=mesh['z'=8,'y'=8,'x'=8,'core'=2] {'x'}, dimensions={0} | all-to-all | bytes 917504 | tf_op jit(solution)/shard_map/all_to_all | solution.py:205
  194.7 13.5 %all_to_all.39 = bf16[8,56,256]{2,1,0:T(8,128)(2,1)S(1)} all-to-all(bf16[8,56,256]{2,1,0:T(8,128)(2,1)S(1)} %broadcast_in_dim.15), channel_id=1, replica_groups=mesh['z'=8,'y'=8,'x'=8,'core'=2] {'x'}, dimensions={0} | all-to-all | bytes 458752 | tf_op jit(solution)/shard_map/all_to_all | solution.py:168
  208.2 2.9 %collective-permute-start.3 = (bf16[448,256]{1,0:T(8,128)(2,1)S(1)}, bf16[448,256]{1,0:T(8,128)(2,1)S(1)}, u32[]{:S(2)}, u32[]{:S(2)}) collective-permute-start(bf16[448,256]{1,0:T(8,128)(2,1)S(1)} %bitcast.24), channel_id=1, source_target_pairs={{0,1},{1,0},{2,3},{3,2},{4,5},{5,4},{6,7},{7,6},{8,9},{9,8},{10,11... | collective-permute-start | bytes 688136 | tf_op jit(solution)/shard_map/ppermute | solution.py:172
  211.2 1.1 collective-permute-done.3.other_ref
  212.3 1.9 shard_map.60
  214.2 0.1 broadcast_in_dim.17
  214.3 16.0 %all_to_all.40 = f32[64,1,512]{2,1,0:T(1,128)S(1)} all-to-all(f32[64,1,512]{2,1,0:T(1,128)S(1)} %broadcast_in_dim.17), channel_id=1, replica_groups=mesh['z'=8,'y'=8,'x'=8,'core'=2] {'z','y'}, dimensions={0} | all-to-all | bytes 262144 | tf_op jit(solution)/shard_map/all_to_all | solution.py:168
  230.3 1.9 shard_map.61
  (7 shorter events, 0.1 us)
Async XLA Ops:
  55.1 33.7 %all-to-all-start.1 = ((f32[64,8,512]{2,1,0:T(8,128)}), f32[64,8,512]{2,1,0:T(8,128)S(1)}, u32[]{:S(2)}, u32[]{:S(2)}) async-start(f32[64,8,512]{2,1,0:T(8,128)} %broadcast_in_dim.12), calls=%async_computation.1 | async-start | bytes 2097152 | tf_op jit(solution)/shard_map/all_to_all | solution.py:168
  91.5 7.5 %collective-permute-start = (f32[8,256]{1,0:T(8,128)S(1)}, f32[8,256]{1,0:T(8,128)S(1)}, u32[]{:S(2)}, u32[]{:S(2)}) collective-permute-start(f32[8,256]{1,0:T(8,128)S(1)} %get-tuple-element.13), channel_id=1, source_target_pairs={{0,1},{1,0},{2,3},{3,2},{4,5},{5,4},{6,7},{7,6},{8,9},{9,8},{10,11... | collective-permute-start | bytes 24584 | tf_op jit(solution)/shard_map/ppermute | solution.py:172
  99.1 43.9 %copy-start = (f32[512,448]{0,1:T(8,128)S(1)}, f32[512,448]{0,1:T(8,128)}, u32[]{:S(2)}) copy-start(f32[512,448]{0,1:T(8,128)} %param.3) | copy-start | bytes 2752516
  112.8 30.1 %copy-start.1 = (bf16[512,448]{0,1:T(8,128)(2,1)S(1)}, bf16[512,448]{0,1:T(8,128)(2,1)}, u32[]{:S(2)}) copy-start(bf16[512,448]{0,1:T(8,128)(2,1)} %param.4) | copy-start | bytes 1376260
  134.4 8.6 %collective-permute-start.1 = (f32[512,256]{1,0:T(8,128)S(1)}, f32[512,256]{1,0:T(8,128)S(1)}, u32[]{:S(2)}, u32[]{:S(2)}) collective-permute-start(f32[512,256]{1,0:T(8,128)S(1)} %bitcast.22), channel_id=1, source_target_pairs={{0,1},{1,0},{2,3},{3,2},{4,5},{5,4},{6,7},{7,6},{8,9},{9,8},{10,11... | collective-permute-start | bytes 1572872 | tf_op jit(solution)/shard_map/ppermute | solution.py:172
  172.0 3.7 %collective-permute-start.2 = (f32[448,256]{1,0:T(8,128)S(1)}, f32[448,256]{1,0:T(8,128)S(1)}, u32[]{:S(2)}, u32[]{:S(2)}) collective-permute-start(f32[448,256]{1,0:T(8,128)S(1)} %get-tuple-element.15), channel_id=1, source_target_pairs={{0,1},{1,0},{2,3},{3,2},{4,5},{5,4},{6,7},{7,6},{8,9},{9,8},{10,11... | collective-permute-start | bytes 1376264 | tf_op jit(solution)/shard_map/ppermute | solution.py:172
  208.2 4.0 %collective-permute-start.3 = (bf16[448,256]{1,0:T(8,128)(2,1)S(1)}, bf16[448,256]{1,0:T(8,128)(2,1)S(1)}, u32[]{:S(2)}, u32[]{:S(2)}) collective-permute-start(bf16[448,256]{1,0:T(8,128)(2,1)S(1)} %bitcast.24), channel_id=1, source_target_pairs={{0,1},{1,0},{2,3},{3,2},{4,5},{5,4},{6,7},{7,6},{8,9},{9,8},{10,11... | collective-permute-start | bytes 688136 | tf_op jit(solution)/shard_map/ppermute | solution.py:172

commit v2 on v1

--- a/solution.py
+++ b/solution.py
@@ -11,7 +11,8 @@
 D = 8192
 FF = 28672
 RANK = 512
-NB = 128
+NB = 64
+TILE = 16
 HALF = RANK // 2
 
 feedback = 0.05
@@ -23,6 +24,11 @@
 SMEM = pl.BlockSpec(memory_space=pltpu.SMEM)
 f32 = jnp.float32
 bf16 = jnp.bfloat16
+ORTHO_SCRATCH = [
+    pltpu.VMEM((RANK, RANK), f32),
+    pltpu.VMEM((RANK, RANK), f32),
+    pltpu.VMEM((NB, 128), f32),
+]
 
 
 def dot(a, b, contract, precision=None):
@@ -62,46 +68,41 @@
 
 
 def row_of(x, k):
-    return jnp.broadcast_to(x[k : k + 1, :], (8, NB))
+    return jnp.broadcast_to(x[k : k + 1, :], x.shape)
 
 
 def lane_of(x, c):
-    return jnp.broadcast_to(x[:, c : c + 1], (8, NB))
-
-
-def diag_inverse(d):
-    sub = lax.broadcasted_iota(jnp.int32, (8, NB), 0)
-    lane = lax.broadcasted_iota(jnp.int32, (8, NB), 1)
-    d = list(d)
-    e = [jnp.where(lane == sub + 8 * i, 1.0, 0.0) for i in range(16)]
+    return jnp.broadcast_to(x[:, c : c + 1], x.shape)
+
+
+def diag_inverse(x, at):
+    sub = lax.broadcasted_iota(jnp.int32, (TILE, 128), 0)
+    x = list(x)
     out = []
-    for t in range(16):
-        s, g, f = d[t], e[t], e[t]
-        cols = [lane_of(s, 8 * t + k) for k in range(8)]
-        pivots = jnp.zeros((8, NB), f32)
-        for k in range(8):
+    for t in range(len(x)):
+        s = f = x[t]
+        cols = [lane_of(s, at + TILE * t + k) for k in range(TILE)]
+        pivots = jnp.zeros((TILE, 128), f32)
+        for k in range(TILE):
             own = sub == k
-            pivot = row_of(cols[k], k)
+            col = cols[k]
+            pivot = row_of(col, k)
             inv = 1.0 / pivot
             pivots = jnp.where(own, pivot, pivots)
-            col = cols[k]
-            for c in range(k + 1, 8):
-                r = row_of(cols[c], k) * inv
-                cols[c] = jnp.where(own, r, cols[c] - col * r)
-            f = jnp.where(sub > k, f - col * (row_of(f, k) * inv), f)
-            if t < 15:
+            for c in range(k + 1, TILE):
+                r = row_of(cols[c], k)
+                cols[c] = jnp.where(own, r * inv, cols[c] - (col * r) * inv)
+            if k < TILE - 1:
+                f = jnp.where(sub > k, f - col * (row_of(f, k) * inv), f)
+            if t < len(x) - 1:
                 r = row_of(s, k) * inv
                 s = jnp.where(own, r, s - col * r)
-                r = row_of(g, k) * inv
-                g = jnp.where(own, r, g - col * r)
         out.append(f * lax.rsqrt(pivots))
-        for i in range(t + 1, 16):
-            di, ei = d[i], e[i]
-            u = [lane_of(d[i], 8 * t + k) for k in range(8)]
-            for k in range(8):
-                di = di - u[k] * row_of(s, k)
-                ei = ei - u[k] * row_of(g, k)
-            d[i], e[i] = di, ei
+        for i in range(t + 1, len(x)):
+            p = [lane_of(x[i], at + TILE * t + k) * row_of(s, k) for k in range(TILE)]
+            while len(p) > 1:
+                p = [p[m] + p[m + 1] for m in range(0, len(p), 2)]
+            x[i] = x[i] - p[0]
     return out
 
 
@@ -113,26 +114,34 @@
     a_ref[:, pl.ds(pl.multiple_of(core * HALF, HALF), HALF)] = own_ref[...]
     a_ref[:, pl.ds(pl.multiple_of((1 - core) * HALF, HALF), HALF)] = other_ref[...]
     l_ref[...] = left_ref[...]
-
-    def outer(j, carry):
-        j0 = pl.multiple_of(j * NB, NB)
-        tiles = [
-            a_ref[pl.ds(pl.multiple_of(j0 + 8 * i, 8), 8), pl.ds(j0, NB)]
-            for i in range(16)
-        ]
-        for i, tile in enumerate(diag_inverse(tiles)):
-            w_ref[8 * i : 8 * i + 8, :] = tile
-        w = w_ref[...]
-        panel = dot(w, a_ref[pl.ds(j0, NB), :], ((1,), (0,)), EXACT)
-        lane = lax.broadcasted_iota(jnp.int32, (NB, RANK), 1)
-        panel = jnp.where(lane >= j0 + NB, panel, 0.0)
-        q = dot(l_ref[:, pl.ds(j0, NB)], w, ((1,), (1,)), EXACT)
-        q_ref[:, pl.ds(j0, NB)] = q.astype(bf16)
-        a_ref[...] -= dot(panel, panel, ((0,), (0,)), EXACT)
-        l_ref[...] -= dot(q, panel, ((1,), (0,)), EXACT)
-        return carry
-
-    lax.fori_loop(0, RANK // NB, outer, 0)
+    sub = lax.broadcasted_iota(jnp.int32, (TILE, 128), 0)
+    lane = lax.broadcasted_iota(jnp.int32, (TILE, 128), 1)
+
+    for j in range(RANK // NB):
+        j0 = j * NB
+        base = j0 // 128 * 128
+        at = j0 - base
+        rest = 64 - at
+        tiles = []
+        for i in range(NB // TILE):
+            a = a_ref[j0 + TILE * i : j0 + TILE * i + TILE, base : base + 128]
+            eye = jnp.where(lane == rest + sub + TILE * i, 1.0, 0.0)
+            tiles.append(jnp.where((lane >= at) & (lane < at + 64), a, eye))
+        for i, tile in enumerate(diag_inverse(tiles, at)):
+            w_ref[TILE * i : TILE * i + TILE, :] = tile
+        w = w_ref[:, rest : rest + 64]
+        if j + 1 < RANK // NB:
+            c0 = (j0 + NB) // 128 * 128
+            panel = dot(w, a_ref[j0 : j0 + NB, c0:], ((1,), (0,)), EXACT)
+            if c0 < j0 + NB:
+                wide = lax.broadcasted_iota(jnp.int32, panel.shape, 1)
+                panel = jnp.where(wide >= j0 + NB - c0, panel, 0.0)
+            a_ref[c0:, c0:] -= dot(panel, panel, ((0,), (0,)), EXACT)
+        q = dot(l_ref[:, j0 : j0 + NB], w, ((1,), (1,)), EXACT)
+        q_ref[:, j0 : j0 + NB] = q.astype(bf16)
+        if j + 1 < RANK // NB:
+            l_ref[:, c0:] -= dot(q, panel, ((1,), (0,)), EXACT)
+
     blend_low = (mom_ref[...] + grad_ref[...].astype(f32)).astype(bf16)
     right = dot(blend_low, q_ref[...], ((1,), (0,)))
     low, high = right[:, :HALF], right[:, HALF:]
@@ -181,6 +190,7 @@
         blended.astype(bf16), factor.astype(bf16), preferred_element_type=f32
     )
     where = jnp.stack([lax.axis_index(ZY), lax.axis_index("core")]).astype(jnp.int32)
+    where, left_part = lax.optimization_barrier((where, left_part))
     mom_t, grad_t = momentum.T, gradient.T
 
     pieces = lax.all_to_all(left_part.reshape(n, rows, RANK), ZY, 0, 0)
@@ -198,7 +208,7 @@
         scratch=[
             pltpu.VMEM((RANK, RANK), f32),
             pltpu.VMEM(left.shape, f32),
-            pltpu.VMEM((NB, NB), f32),
+            pltpu.VMEM((NB, 128), f32),
         ],
     )
     part = (keep + swap(send)).reshape(nx, width // nx, HALF)

time: 233 us -> 223 us (0.957)
  blocking collectives: 135 us -> 168 us
  waiting for transfers between devices: 30.7 us -> 4.67 us
  Pallas kernels: 35.6 us -> 27 us
  starting transfers between devices: 26.7 us -> 19.1 us
    all_to_all x4 -> x5, blocking collectives: 64.7 us -> 98.2 us  [to_all(): return lax.all_to_all(jnp.broadcast_to(x[None], (n,) + x.shape), axes, 0, 0)]
    all_to_all x1 -> x0, waiting for transfers between devices: 25.8 us -> none  [to_all(): return lax.all_to_all(jnp.broadcast_to(x[None], (n,) + x.shape), axes, 0, 0)]
    pallas_call x4, Pallas kernels: 35.6 us -> 27 us  [call(): pl.pallas_call(kernel, out_shape=outs, in_specs=specs, out_specs=jax.tree...]
    all_to_all x1 -> x0, starting transfers between devices: 7.72 us -> none  [to_all(): return lax.all_to_all(jnp.broadcast_to(x[None], (n,) + x.shape), axes, 0, 0)]
  transfers between devices with their start and end apart: 5 -> 4, of which waited for: 5 -> 4; matrix products, arithmetic and copies ran while one was open for 0% -> 0% of each run, Pallas kernels for 0% -> 0%
where the time goes in v2:
time: 223 us; the launch traced here: 222 us
  blocking collectives  168 us (75%)
  Pallas kernels  27 us (12%)
  starting transfers between devices  19.1 us (9%)
  waiting for transfers between devices  4.67 us (2%)
    all_to_all x5, blocking collectives, to_all(): return lax.all_to_all(jnp.broadcast_to(x[None], (n,) + x.shape), axes, 0, 0)  98.2 us
    all_to_all x1, blocking collectives, per_device(): pieces = lax.all_to_all(left_part.reshape(n, rows, RANK), ZY, 0, 0)  51.2 us
    pallas_call x4, Pallas kernels, call(): pl.pallas_call(kernel, out_shape=outs, in_specs=specs, out_specs=jax.tree...  27 us
    ppermute x4, starting transfers between devices, swap(): return lax.ppermute(x, 'core', [(0, 1), (1, 0)])  19.1 us
    all_to_all x1, blocking collectives, per_device(): mine = jnp.sum(lax.all_to_all(part, 'x', 0, 0), axis=0).astype(bf16)  19 us
    ppermute x4, waiting for transfers between devices, swap(): return lax.ppermute(x, 'core', [(0, 1), (1, 0)])  4.67 us
  transfers between devices with their start and end apart: 4, of which 4 were waited for; matrix products, arithmetic and copies ran while one was open for 0% of the time, Pallas kernels for 0%

profile of v2, /device:TPU:1, one launch (start us, length us, event | category | flops | bytes accessed | tf_op | source)
XLA Modules:
  0.0 222.5 jit_solution(8793555491730514255)
XLA Ops:
  0.6 0.1 pad_add_fusion.where_ref
  0.7 2.1 fusion
  2.8 51.2 %all_to_all.35 = f32[64,8,512]{2,1,0:T(8,128)S(1)} all-to-all(f32[64,8,512]{2,1,0:T(8,128)S(1)} %bitcast.28), channel_id=1, replica_groups=mesh['z'=8,'y'=8,'x'=8,'core'=2] {'z','y'}, dimensions={0} | all-to-all | bytes 2097152 | tf_op jit(solution)/shard_map/all_to_all | solution.py:196
  54.0 0.1 reduce_sum.27
  54.1 0.1 broadcast_in_dim.12
  54.2 33.4 %all_to_all.36 = f32[64,8,512]{2,1,0:T(8,128)S(1)} all-to-all(f32[64,8,512]{2,1,0:T(8,128)S(1)} %broadcast_in_dim.12), channel_id=1, replica_groups=mesh['z'=8,'y'=8,'x'=8,'core'=2] {'z','y'}, dimensions={0} | all-to-all | bytes 2097152 | tf_op jit(solution)/shard_map/all_to_all | solution.py:177
  87.7 2.8 %shard_map.58 = (f32[8,256]{1,0:T(8,128)S(1)}, f32[8,256]{1,0:T(8,128)S(1)}) custom-call(s32[2]{0:T(128)S(1)} %pad_add_fusion.where_ref, f32[512,512]{1,0:T(8,128)S(1)} %bitcast.15), custom_call_target="tpu_custom_call" | custom-call | tf_op jit(solution)/shard_map/pallas_call | solution.py:42
  90.4 6.7 %collective-permute-start = (f32[8,256]{1,0:T(8,128)S(1)}, f32[8,256]{1,0:T(8,128)S(1)}, u32[]{:S(2)}, u32[]{:S(2)}) collective-permute-start(f32[8,256]{1,0:T(8,128)S(1)} %get-tuple-element.17), channel_id=1, source_target_pairs={{0,1},{1,0},{2,3},{3,2},{4,5},{5,4},{6,7},{7,6},{8,9},{9,8},{10,11... | collective-permute-start | bytes 24584 | tf_op jit(solution)/shard_map/ppermute | solution.py:181
  97.1 0.8 collective-permute-done
  98.0 0.0 copy-start
  98.0 13.6 %all_to_all.37 = f32[8,8,256]{2,1,0:T(8,128)S(1)} all-to-all(f32[8,8,256]{2,1,0:T(8,128)S(1)} %broadcast_in_dim.13), channel_id=1, replica_groups=mesh['z'=8,'y'=8,'x'=8,'core'=2] {'x'}, dimensions={0} | all-to-all | bytes 131072 | tf_op jit(solution)/shard_map/all_to_all | solution.py:177
  111.7 0.0 copy-start.1
  111.7 21.6 %all_to_all.38 = f32[64,8,256]{2,1,0:T(8,128)S(1)} all-to-all(f32[64,8,256]{2,1,0:T(8,128)S(1)} %broadcast_in_dim.14), channel_id=1, replica_groups=mesh['z'=8,'y'=8,'x'=8,'core'=2] {'z','y'}, dimensions={0} | all-to-all | bytes 1048576 | tf_op jit(solution)/shard_map/all_to_all | solution.py:177
  133.2 7.2 %collective-permute-start.1 = (f32[512,256]{1,0:T(8,128)S(1)}, f32[512,256]{1,0:T(8,128)S(1)}, u32[]{:S(2)}, u32[]{:S(2)}) collective-permute-start(f32[512,256]{1,0:T(8,128)S(1)} %bitcast.21), channel_id=1, source_target_pairs={{0,1},{1,0},{2,3},{3,2},{4,5},{5,4},{6,7},{7,6},{8,9},{9,8},{10,11... | collective-permute-start | bytes 1572872 | tf_op jit(solution)/shard_map/ppermute | solution.py:181
  140.5 1.3 collective-permute-done.1.other_ref
  141.8 0.0 copy-done
  141.8 0.0 copy-done.1
  141.8 20.4 %shard_map.59 = (bf16[512,512]{1,0:T(8,128)(2,1)S(1)}, f32[448,256]{1,0:T(8,128)S(1)}, f32[448,256]{1,0:T(8,128)S(1)}) custom-call(s32[2]{0:T(128)S(1)} %pad_add_fusion.where_ref, f32[512,256]{1,0:T(8,128)S(1)} %bitcast.22, f32[512,256]{1,0:T(8,128)S(1)} %collective-permute-done.1.other_ref, f32[512,512]{1,0:T(8,128)S(1)} %bitcast.16, ...), custom_call_target="tpu_custom_call" | custom-call | tf_op jit(solution)/shard_map/pallas_call | solution.py:42
  162.2 2.3 %collective-permute-start.2 = (f32[448,256]{1,0:T(8,128)S(1)}, f32[448,256]{1,0:T(8,128)S(1)}, u32[]{:S(2)}, u32[]{:S(2)}) collective-permute-start(f32[448,256]{1,0:T(8,128)S(1)} %get-tuple-element.19), channel_id=1, source_target_pairs={{0,1},{1,0},{2,3},{3,2},{4,5},{5,4},{6,7},{7,6},{8,9},{9,8},{10,11... | collective-permute-start | bytes 1376264 | tf_op jit(solution)/shard_map/ppermute | solution.py:181
  164.5 1.4 collective-permute-done.2
  166.0 0.1 add.15
  166.0 19.0 %all_to_all.39 = f32[8,56,256]{2,1,0:T(8,128)S(1)} all-to-all(f32[8,56,256]{2,1,0:T(8,128)S(1)} %bitcast.29), channel_id=1, replica_groups=mesh['z'=8,'y'=8,'x'=8,'core'=2] {'x'}, dimensions={0} | all-to-all | bytes 917504 | tf_op jit(solution)/shard_map/all_to_all | solution.py:215
  185.0 13.5 %all_to_all.40 = bf16[8,56,256]{2,1,0:T(8,128)(2,1)S(1)} all-to-all(bf16[8,56,256]{2,1,0:T(8,128)(2,1)S(1)} %broadcast_in_dim.15), channel_id=1, replica_groups=mesh['z'=8,'y'=8,'x'=8,'core'=2] {'x'}, dimensions={0} | all-to-all | bytes 458752 | tf_op jit(solution)/shard_map/all_to_all | solution.py:177
  198.5 2.9 %collective-permute-start.3 = (bf16[448,256]{1,0:T(8,128)(2,1)S(1)}, bf16[448,256]{1,0:T(8,128)(2,1)S(1)}, u32[]{:S(2)}, u32[]{:S(2)}) collective-permute-start(bf16[448,256]{1,0:T(8,128)(2,1)S(1)} %bitcast.23), channel_id=1, source_target_pairs={{0,1},{1,0},{2,3},{3,2},{4,5},{5,4},{6,7},{7,6},{8,9},{9,8},{10,11... | collective-permute-start | bytes 688136 | tf_op jit(solution)/shard_map/ppermute | solution.py:181
  201.5 1.1 collective-permute-done.3.other_ref
  202.6 1.9 shard_map.60
  204.5 0.1 broadcast_in_dim.17
  204.5 16.1 %all_to_all.41 = f32[64,1,512]{2,1,0:T(1,128)S(1)} all-to-all(f32[64,1,512]{2,1,0:T(1,128)S(1)} %broadcast_in_dim.17), channel_id=1, replica_groups=mesh['z'=8,'y'=8,'x'=8,'core'=2] {'z','y'}, dimensions={0} | all-to-all | bytes 262144 | tf_op jit(solution)/shard_map/all_to_all | solution.py:177
  220.6 1.9 shard_map.61
  (7 shorter events, 0.1 us)
Async XLA Ops:
  90.4 7.5 %collective-permute-start = (f32[8,256]{1,0:T(8,128)S(1)}, f32[8,256]{1,0:T(8,128)S(1)}, u32[]{:S(2)}, u32[]{:S(2)}) collective-permute-start(f32[8,256]{1,0:T(8,128)S(1)} %get-tuple-element.17), channel_id=1, source_target_pairs={{0,1},{1,0},{2,3},{3,2},{4,5},{5,4},{6,7},{7,6},{8,9},{9,8},{10,11... | collective-permute-start | bytes 24584 | tf_op jit(solution)/shard_map/ppermute | solution.py:181
  98.0 43.8 %copy-start = (f32[512,448]{0,1:T(8,128)S(1)}, f32[512,448]{0,1:T(8,128)}, u32[]{:S(2)}) copy-start(f32[512,448]{0,1:T(8,128)} %param.3) | copy-start | bytes 2752516
  111.7 30.1 %copy-start.1 = (bf16[512,448]{0,1:T(8,128)(2,1)S(1)}, bf16[512,448]{0,1:T(8,128)(2,1)}, u32[]{:S(2)}) copy-start(bf16[512,448]{0,1:T(8,128)(2,1)} %param.4) | copy-start | bytes 1376260
  133.2 8.6 %collective-permute-start.1 = (f32[512,256]{1,0:T(8,128)S(1)}, f32[512,256]{1,0:T(8,128)S(1)}, u32[]{:S(2)}, u32[]{:S(2)}) collective-permute-start(f32[512,256]{1,0:T(8,128)S(1)} %bitcast.21), channel_id=1, source_target_pairs={{0,1},{1,0},{2,3},{3,2},{4,5},{5,4},{6,7},{7,6},{8,9},{9,8},{10,11... | collective-permute-start | bytes 1572872 | tf_op jit(solution)/shard_map/ppermute | solution.py:181
  162.2 3.7 %collective-permute-start.2 = (f32[448,256]{1,0:T(8,128)S(1)}, f32[448,256]{1,0:T(8,128)S(1)}, u32[]{:S(2)}, u32[]{:S(2)}) collective-permute-start(f32[448,256]{1,0:T(8,128)S(1)} %get-tuple-element.19), channel_id=1, source_target_pairs={{0,1},{1,0},{2,3},{3,2},{4,5},{5,4},{6,7},{7,6},{8,9},{9,8},{10,11... | collective-permute-start | bytes 1376264 | tf_op jit(solution)/shard_map/ppermute | solution.py:181
  198.5 4.0 %collective-permute-start.3 = (bf16[448,256]{1,0:T(8,128)(2,1)S(1)}, bf16[448,256]{1,0:T(8,128)(2,1)S(1)}, u32[]{:S(2)}, u32[]{:S(2)}) collective-permute-start(bf16[448,256]{1,0:T(8,128)(2,1)S(1)} %bitcast.23), channel_id=1, source_target_pairs={{0,1},{1,0},{2,3},{3,2},{4,5},{5,4},{6,7},{7,6},{8,9},{9,8},{10,11... | collective-permute-start | bytes 688136 | tf_op jit(solution)/shard_map/ppermute | solution.py:181

commit v3 on v2

--- a/solution.py
+++ b/solution.py
@@ -53,7 +53,7 @@
     return jax.ShapeDtypeStruct(dims, dtype)
 
 
-def gram_kernel(where_ref, left_ref, keep_ref, send_ref):
+def gram_kernel(where_ref, left_ref, halves_ref):
     left = left_ref[...]
     first = where_ref[0] * 8
     row = lax.broadcasted_iota(jnp.int32, (RANK, 8), 0)
@@ -61,10 +61,8 @@
     pick = jnp.where(row == first + col, 1.0, 0.0)
     columns = dot(left, pick, ((1,), (0,)), EXACT)
     rows = dot(columns, left, ((0,), (0,)), EXACT)
-    own_low = where_ref[1] == 0
-    low, high = rows[:, :HALF], rows[:, HALF:]
-    keep_ref[...] = jnp.where(own_low, low, high)
-    send_ref[...] = jnp.where(own_low, high, low)
+    halves_ref[0] = rows[:, :HALF]
+    halves_ref[1] = rows[:, HALF:]
 
 
 def row_of(x, k):
@@ -149,28 +147,37 @@
     send_ref[...] = jnp.where(core == 0, high, low)
 
 
-def whole(core, own_ref, other_ref):
-    own, other = own_ref[...], other_ref[...]
-    first = jnp.where(core == 0, own, other)
-    second = jnp.where(core == 0, other, own)
-    return jnp.concatenate([first, second], axis=1)
-
-
-def momentum_kernel(where_ref, own_ref, other_ref, q_ref, mom_ref, grad_ref, out_ref, squares_ref):
-    right = whole(where_ref[1], own_ref, other_ref)
-    feed = dot(right, q_ref[...], ((1,), (1,)))
+def momentum_kernel(right_ref, q_ref, mom_ref, grad_ref, out_ref, squares_ref):
+    right = right_ref[...]
+    feed = dot(right.astype(bf16), q_ref[...], ((1,), (1,)))
     out_ref[...] = mom_ref[...] + grad_ref[...].astype(f32) - feedback * feed
-    wide = right.astype(f32)
-    squares_ref[...] = jnp.sum(wide * wide, axis=0, keepdims=True)
-
-
-def update_kernel(where_ref, own_ref, other_ref, q_ref, squares_ref, factor_ref, update_ref):
-    right = whole(where_ref[1], own_ref, other_ref).astype(f32)
+    squares_ref[...] = jnp.sum(right * right, axis=0, keepdims=True)
+
+
+def update_kernel(right_ref, q_ref, squares_ref, factor_ref, update_ref):
     mean = jnp.sum(squares_ref[...], axis=0, keepdims=True) / FF
-    factor_new = right / jnp.sqrt(mean + epsilon)
+    factor_new = right_ref[...] / jnp.sqrt(mean + epsilon)
     factor_ref[...] = factor_new
     update = dot(factor_new.astype(bf16), q_ref[...], ((1,), (1,)))
     update_ref[...] = (math.sqrt(D / RANK) * update).astype(bf16)
+
+
+def enc(x, scale, knee):
+    x = x * scale
+    size = jnp.abs(x)
+    root = jnp.sqrt(size * knee)
+    return jnp.where(size < knee, jnp.where(x < 0, -root, root), x).astype(jnp.float16)
+
+
+def dec(x, scale, knee):
+    x = x.astype(f32)
+    size = jnp.abs(x)
+    return jnp.where(size < knee, x * size * (1.0 / knee), x) * (1.0 / scale)
+
+
+PART = (2.0**-2, 0.25)
+LEFT = (2.0**-8, 0.125)
+RIGHT = (2.0**3, 0.25)
 
 
 def to_all(x, axes, n):
@@ -189,15 +196,18 @@
     left_part = jnp.dot(
         blended.astype(bf16), factor.astype(bf16), preferred_element_type=f32
     )
-    where = jnp.stack([lax.axis_index(ZY), lax.axis_index("core")]).astype(jnp.int32)
+    core = lax.axis_index("core")
+    where = jnp.stack([lax.axis_index(ZY), core]).astype(jnp.int32)
     where, left_part = lax.optimization_barrier((where, left_part))
     mom_t, grad_t = momentum.T, gradient.T
 
-    pieces = lax.all_to_all(left_part.reshape(n, rows, RANK), ZY, 0, 0)
-    left = to_all(jnp.sum(pieces, axis=0), ZY, n).reshape(n * rows, RANK)
-
-    keep, send = call(gram_kernel, (shape((8, HALF), f32),) * 2, where, left)
-    gram_rows = jnp.sum(to_all(keep + swap(send), "x", nx), axis=0)
+    pieces = lax.all_to_all(enc(left_part, *PART).reshape(n, rows, RANK), ZY, 0, 0)
+    share = enc(jnp.sum(dec(pieces, *PART), axis=0), *LEFT)
+    left = dec(to_all(share, ZY, n), *LEFT).reshape(n * rows, RANK)
+
+    halves = call(gram_kernel, shape((2, 8, HALF), f32), where, left)
+    halves = jnp.broadcast_to(halves[None], (nx, 2, 8, HALF)).reshape(2 * nx, 8, HALF)
+    gram_rows = jnp.sum(lax.all_to_all(halves, ("x", "core"), 0, 0), axis=0)
     gram_own = to_all(gram_rows, ZY, n).reshape(RANK, HALF)
     gram_other = swap(gram_own)
 
@@ -205,27 +215,26 @@
         ortho_kernel,
         (shape(left.shape, bf16),) + (shape((width, HALF), f32),) * 2,
         where, gram_own, gram_other, left, mom_t, grad_t,
-        scratch=[
-            pltpu.VMEM((RANK, RANK), f32),
-            pltpu.VMEM(left.shape, f32),
-            pltpu.VMEM((NB, 128), f32),
-        ],
-    )
-    part = (keep + swap(send)).reshape(nx, width // nx, HALF)
-    mine = jnp.sum(lax.all_to_all(part, "x", 0, 0), axis=0).astype(bf16)
-    own = to_all(mine, "x", nx).reshape(width, HALF)
+        scratch=ORTHO_SCRATCH,
+    )
+    part = enc(keep + swap(send), *RIGHT).reshape(nx, width // nx, HALF)
+    mine = jnp.sum(dec(lax.all_to_all(part, "x", 0, 0), *RIGHT), axis=0)
+    own = to_all(enc(mine, *RIGHT), "x", nx).reshape(width, HALF)
     other = swap(own)
+    low = jnp.where(core == 0, own, other)
+    high = jnp.where(core == 0, other, own)
+    right = dec(jnp.concatenate([low, high], axis=1), *RIGHT)
 
     momentum_t, squares = call(
         momentum_kernel,
         (shape((width, left.shape[0]), f32), shape((1, RANK), f32)),
-        where, own, other, left_low, mom_t, grad_t,
+        right, left_low, mom_t, grad_t,
     )
     squares = to_all(squares, ZY, n).reshape(n, RANK)
     factor_new, update_t = call(
         update_kernel,
         (shape((width, RANK), f32), shape((width, left.shape[0]), bf16)),
-        where, own, other, left_low, squares,
+        right, left_low, squares,
     )
     return (momentum_t.T, factor_new, update_t.T)
 

time: 223 us -> 196 us (0.88)
  blocking collectives: 168 us -> 149 us
  starting transfers between devices: 19.1 us -> 10.8 us
    all_to_all x5 -> x4, blocking collectives: 98.2 us -> 74.8 us  [to_all(): return lax.all_to_all(jnp.broadcast_to(x[None], (n,) + x.shape), axes, 0, 0)]
    ppermute x4 -> x3, starting transfers between devices: 19.1 us -> 10.8 us  [swap(): return lax.ppermute(x, 'core', [(0, 1), (1, 0)])]
    all_to_all x2 -> x3, blocking collectives: 70.2 us -> 74.4 us  [the longest x1 40.9 us: per_device(): lax.all_to_all(enc(left_part, *PART).reshape(n, rows, RANK), ZY, 0, 0)]
    ppermute x4 -> x3, waiting for transfers between devices: 4.67 us -> 3.86 us  [swap(): return lax.ppermute(x, 'core', [(0, 1), (1, 0)])]
  transfers between devices with their start and end apart: 4 -> 3, of which waited for: 4 -> 3; matrix products, arithmetic and copies ran while one was open for 0% -> 0% of each run, Pallas kernels for 0% -> 0%
where the time goes in v3:
time: 196 us; the launch traced here: 195 us
  blocking collectives  149 us (76%)
  Pallas kernels  25.9 us (13%)
  starting transfers between devices  10.8 us (6%)
  waiting for transfers between devices  3.86 us (2%)
  other arithmetic  2.12 us (1%)
  matrix products  2.08 us (1%)
    all_to_all x4, blocking collectives, to_all(): return lax.all_to_all(jnp.broadcast_to(x[None], (n,) + x.shape), axes, 0, 0)  74.8 us
    all_to_all x1, blocking collectives, per_device(): lax.all_to_all(enc(left_part, *PART).reshape(n, rows, RANK), ZY, 0, 0)  40.9 us
    pallas_call x4, Pallas kernels, call(): pl.pallas_call(kernel, out_shape=outs, in_specs=specs, out_specs=jax.tree...  25.9 us
    all_to_all x1, blocking collectives, per_device(): gram_rows = jnp.sum(lax.all_to_all(halves, ('x', 'core'), 0, 0), axis=0)  20.4 us
    all_to_all x1, blocking collectives, per_device(): mine = jnp.sum(dec(lax.all_to_all(part, 'x', 0, 0), *RIGHT), axis=0)  13.1 us
    ppermute x3, starting transfers between devices, swap(): return lax.ppermute(x, 'core', [(0, 1), (1, 0)])  10.8 us
  transfers between devices with their start and end apart: 3, of which 3 were waited for; matrix products, arithmetic and copies ran while one was open for 0% of the time, Pallas kernels for 0%

profile of v3, /device:TPU:1, one launch (start us, length us, event | category | flops | bytes accessed | tf_op | source)
XLA Modules:
  0.0 195.0 jit_solution(17882900620415260747)
XLA Ops:
  0.6 0.1 pad_add_fusion.where_ref
  0.7 2.1 %fusion.20 = f32[512,512]{1,0:T(8,128)S(1)} fusion(f32[512,448]{0,1:T(8,128)} %param.3, bf16[512,448]{0,1:T(8,128)(2,1)} %param.4, f32[448,512]{1,0:T(8,128)} %param.5), kind=kOutput, calls=%fused_computation.35 | convolution fusion | flops 235798528 | bytes 3342336 | tf_op jit(solution)/shard_map/dot_general | solution.py:196
  2.8 0.7 fusion.14
  3.5 40.9 %all_to_all.35 = f16[64,8,512]{2,1,0:T(8,128)(2,1)S(1)} all-to-all(f16[64,8,512]{2,1,0:T(8,128)(2,1)S(1)} %fusion.14), channel_id=1, replica_groups=mesh['z'=8,'y'=8,'x'=8,'core'=2] {'z','y'}, dimensions={0} | all-to-all | bytes 1048576 | tf_op jit(solution)/shard_map/all_to_all | solution.py:204
  44.4 0.3 fusion.7
  44.7 22.5 %all_to_all.36 = f16[64,8,512]{2,1,0:T(8,128)(2,1)S(1)} all-to-all(f16[64,8,512]{2,1,0:T(8,128)(2,1)S(1)} %broadcast_in_dim.12), channel_id=1, replica_groups=mesh['z'=8,'y'=8,'x'=8,'core'=2] {'z','y'}, dimensions={0} | all-to-all | bytes 1048576 | tf_op jit(solution)/shard_map/all_to_all | solution.py:184
  67.2 0.2 fusion.10.left_ref
  67.5 2.8 %shard_map.58 = f32[2,8,256]{2,1,0:T(8,128)S(1)} custom-call(s32[2]{0:T(128)S(1)} %pad_add_fusion.where_ref, f32[512,512]{1,0:T(8,128)S(1)} %fusion.10.left_ref), custom_call_target="tpu_custom_call" | custom-call | tf_op jit(solution)/shard_map/pallas_call | solution.py:42
  70.3 20.4 %all_to_all.37 = f32[16,8,256]{2,1,0:T(8,128)S(1)} all-to-all(f32[16,8,256]{2,1,0:T(8,128)S(1)} %bitcast.30), channel_id=1, replica_groups=mesh['z'=8,'y'=8,'x'=8,'core'=2] {'x','core'}, dimensions={0} | all-to-all | bytes 262144 | tf_op jit(solution)/shard_map/all_to_all | solution.py:210
  90.6 0.0 copy-start
  90.7 0.0 copy-start.1
  90.7 22.8 %all_to_all.38 = f32[64,8,256]{2,1,0:T(8,128)S(1)} all-to-all(f32[64,8,256]{2,1,0:T(8,128)S(1)} %broadcast_in_dim.14), channel_id=1, replica_groups=mesh['z'=8,'y'=8,'x'=8,'core'=2] {'z','y'}, dimensions={0} | all-to-all | bytes 1048576 | tf_op jit(solution)/shard_map/all_to_all | solution.py:184
  113.5 3.4 %collective-permute-start = (f32[512,256]{1,0:T(8,128)S(1)}, f32[512,256]{1,0:T(8,128)S(1)}, u32[]{:S(2)}, u32[]{:S(2)}) collective-permute-start(f32[512,256]{1,0:T(8,128)S(1)} %bitcast.24), channel_id=1, source_target_pairs={{0,1},{1,0},{2,3},{3,2},{4,5},{5,4},{6,7},{7,6},{8,9},{9,8},{10,11... | collective-permute-start | bytes 1572872 | tf_op jit(solution)/shard_map/ppermute | solution.py:188
  116.9 1.3 collective-permute-done.other_ref
  118.2 0.0 copy-done
  118.2 0.0 copy-done.1
  118.2 20.4 %shard_map.59 = (bf16[512,512]{1,0:T(8,128)(2,1)S(1)}, f32[448,256]{1,0:T(8,128)S(1)}, f32[448,256]{1,0:T(8,128)S(1)}) custom-call(s32[2]{0:T(128)S(1)} %pad_add_fusion.where_ref, f32[512,256]{1,0:T(8,128)S(1)} %bitcast.25, f32[512,256]{1,0:T(8,128)S(1)} %collective-permute-done.other_ref, f32[512,512]{1,0:T(8,128)S(1)} %fusion.10.left_ref, ...), custom_call_target="tpu_custom_call" | custom-call | tf_op jit(solution)/shard_map/pallas_call | solution.py:42
  138.7 2.3 %collective-permute-start.1 = (f32[448,256]{1,0:T(8,128)S(1)}, f32[448,256]{1,0:T(8,128)S(1)}, u32[]{:S(2)}, u32[]{:S(2)}) collective-permute-start(f32[448,256]{1,0:T(8,128)S(1)} %get-tuple-element.15), channel_id=1, source_target_pairs={{0,1},{1,0},{2,3},{3,2},{4,5},{5,4},{6,7},{7,6},{8,9},{9,8},{10,11... | collective-permute-start | bytes 1376264 | tf_op jit(solution)/shard_map/ppermute | solution.py:188
  140.9 1.4 collective-permute-done.1
  142.4 0.3 fusion.16
  142.7 13.1 %all_to_all.39 = f16[8,56,256]{2,1,0:T(8,128)(2,1)S(1)} all-to-all(f16[8,56,256]{2,1,0:T(8,128)(2,1)S(1)} %bitcast.29), channel_id=1, replica_groups=mesh['z'=8,'y'=8,'x'=8,'core'=2] {'x'}, dimensions={0} | all-to-all | bytes 458752 | tf_op jit(solution)/shard_map/all_to_all | solution.py:221
  155.8 0.1 fusion.19
  156.0 11.3 %all_to_all.40 = f16[8,56,256]{2,1,0:T(8,128)(2,1)S(1)} all-to-all(f16[8,56,256]{2,1,0:T(8,128)(2,1)S(1)} %broadcast_in_dim.15), channel_id=1, replica_groups=mesh['z'=8,'y'=8,'x'=8,'core'=2] {'x'}, dimensions={0} | all-to-all | bytes 458752 | tf_op jit(solution)/shard_map/all_to_all | solution.py:184
  167.3 5.2 %collective-permute-start.2 = (f16[448,256]{1,0:T(8,128)(2,1)S(1)}, f16[448,256]{1,0:T(8,128)(2,1)S(1)}, u32[]{:S(2)}, u32[]{:S(2)}) collective-permute-start(f16[448,256]{1,0:T(8,128)(2,1)S(1)} %bitcast.28), channel_id=1, source_target_pairs={{0,1},{1,0},{2,3},{3,2},{4,5},{5,4},{6,7},{7,6},{8,9},{9,8},{10,11... | collective-permute-start | bytes 688136 | tf_op jit(solution)/shard_map/ppermute | solution.py:188
  172.5 1.1 collective-permute-done.2
  173.6 0.1 broadcast_select_fusion.1
  173.7 0.2 fusion.12.right_ref
  174.0 1.4 shard_map.60
  175.3 0.1 broadcast_in_dim.17
  175.4 18.3 %all_to_all.41 = f32[64,1,512]{2,1,0:T(1,128)S(1)} all-to-all(f32[64,1,512]{2,1,0:T(1,128)S(1)} %broadcast_in_dim.17), channel_id=1, replica_groups=mesh['z'=8,'y'=8,'x'=8,'core'=2] {'z','y'}, dimensions={0} | all-to-all | bytes 262144 | tf_op jit(solution)/shard_map/all_to_all | solution.py:184
  193.7 1.3 shard_map.61
  (8 shorter events, 0.2 us)
Async XLA Ops:
  90.6 27.6 %copy-start = (f32[512,448]{0,1:T(8,128)S(1)}, f32[512,448]{0,1:T(8,128)}, u32[]{:S(2)}) copy-start(f32[512,448]{0,1:T(8,128)} %param.3) | copy-start | bytes 2752516
  90.7 27.5 %copy-start.1 = (bf16[512,448]{0,1:T(8,128)(2,1)S(1)}, bf16[512,448]{0,1:T(8,128)(2,1)}, u32[]{:S(2)}) copy-start(bf16[512,448]{0,1:T(8,128)(2,1)} %param.4) | copy-start | bytes 1376260
  113.5 4.7 %collective-permute-start = (f32[512,256]{1,0:T(8,128)S(1)}, f32[512,256]{1,0:T(8,128)S(1)}, u32[]{:S(2)}, u32[]{:S(2)}) collective-permute-start(f32[512,256]{1,0:T(8,128)S(1)} %bitcast.24), channel_id=1, source_target_pairs={{0,1},{1,0},{2,3},{3,2},{4,5},{5,4},{6,7},{7,6},{8,9},{9,8},{10,11... | collective-permute-start | bytes 1572872 | tf_op jit(solution)/shard_map/ppermute | solution.py:188
  138.7 3.7 %collective-permute-start.1 = (f32[448,256]{1,0:T(8,128)S(1)}, f32[448,256]{1,0:T(8,128)S(1)}, u32[]{:S(2)}, u32[]{:S(2)}) collective-permute-start(f32[448,256]{1,0:T(8,128)S(1)} %get-tuple-element.15), channel_id=1, source_target_pairs={{0,1},{1,0},{2,3},{3,2},{4,5},{5,4},{6,7},{7,6},{8,9},{9,8},{10,11... | collective-permute-start | bytes 1376264 | tf_op jit(solution)/shard_map/ppermute | solution.py:188
  167.3 6.3 %collective-permute-start.2 = (f16[448,256]{1,0:T(8,128)(2,1)S(1)}, f16[448,256]{1,0:T(8,128)(2,1)S(1)}, u32[]{:S(2)}, u32[]{:S(2)}) collective-permute-start(f16[448,256]{1,0:T(8,128)(2,1)S(1)} %bitcast.28), channel_id=1, source_target_pairs={{0,1},{1,0},{2,3},{3,2},{4,5},{5,4},{6,7},{7,6},{8,9},{9,8},{10,11... | collective-permute-start | bytes 688136 | tf_op jit(solution)/shard_map/ppermute | solution.py:188

commit v4 on v3

--- a/solution.py
+++ b/solution.py
@@ -53,54 +53,77 @@
     return jax.ShapeDtypeStruct(dims, dtype)
 
 
-def gram_kernel(where_ref, left_ref, halves_ref):
-    left = left_ref[...]
-    first = where_ref[0] * 8
-    row = lax.broadcasted_iota(jnp.int32, (RANK, 8), 0)
-    col = lax.broadcasted_iota(jnp.int32, (RANK, 8), 1)
-    pick = jnp.where(row == first + col, 1.0, 0.0)
-    columns = dot(left, pick, ((1,), (0,)), EXACT)
-    rows = dot(columns, left, ((0,), (0,)), EXACT)
+def gram_kernel(where_ref, left_ref, halves_ref, turned_ref):
+    group, first = where_ref[0] // 16, where_ref[0] % 16 * 8
+    turned_ref[...] = left_ref[:, pl.ds(pl.multiple_of(group * 128, 128), 128)].T
+    columns = turned_ref[pl.ds(pl.multiple_of(first, 8), 8), :]
+    rows = dot(columns, left_ref[...], ((1,), (0,)), EXACT)
     halves_ref[0] = rows[:, :HALF]
     halves_ref[1] = rows[:, HALF:]
 
 
 def row_of(x, k):
-    return jnp.broadcast_to(x[k : k + 1, :], x.shape)
+    return jnp.broadcast_to(x[k // 8][k % 8 : k % 8 + 1, :], (8, 128))
 
 
 def lane_of(x, c):
-    return jnp.broadcast_to(x[:, c : c + 1], x.shape)
-
-
-def diag_inverse(x, at):
-    sub = lax.broadcasted_iota(jnp.int32, (TILE, 128), 0)
+    return [jnp.broadcast_to(h[:, c : c + 1], (8, 128)) for h in x]
+
+
+def diag_inverse(x, at, fill=None):
+    sub = lax.broadcasted_iota(jnp.int32, (8, 128), 0)
     x = list(x)
     out = []
+
+    def below(old, m, r, k, done):
+        new = [h - a * r for h, a in zip(old, m)]
+        new[k // 8] = jnp.where(sub == k % 8, done, new[k // 8])
+        return new
+
     for t in range(len(x)):
         s = f = x[t]
         cols = [lane_of(s, at + TILE * t + k) for k in range(TILE)]
-        pivots = jnp.zeros((TILE, 128), f32)
+        pivots = [jnp.zeros((8, 128), f32)] * 2
         for k in range(TILE):
-            own = sub == k
             col = cols[k]
             pivot = row_of(col, k)
             inv = 1.0 / pivot
-            pivots = jnp.where(own, pivot, pivots)
+            pivots[k // 8] = jnp.where(sub == k % 8, pivot, pivots[k // 8])
+            m = [h * inv for h in col]
             for c in range(k + 1, TILE):
                 r = row_of(cols[c], k)
-                cols[c] = jnp.where(own, r * inv, cols[c] - (col * r) * inv)
+                if c == k + 1:
+                    new = [h - (a * r) * inv for h, a in zip(cols[c], col)]
+                    new[k // 8] = jnp.where(sub == k % 8, r * inv, new[k // 8])
+                    cols[c] = new
+                else:
+                    cols[c] = below(cols[c], m, r, k, r * inv)
             if k < TILE - 1:
-                f = jnp.where(sub > k, f - col * (row_of(f, k) * inv), f)
+                r = row_of(f, k)
+                new = list(f)
+                if k < 7:
+                    new[0] = jnp.where(sub > k, f[0] - m[0] * r, f[0])
+                if k < 8:
+                    new[1] = f[1] - m[1] * r
+                else:
+                    new[1] = jnp.where(sub > k - 8, f[1] - m[1] * r, f[1])
+                f = new
             if t < len(x) - 1:
-                r = row_of(s, k) * inv
-                s = jnp.where(own, r, s - col * r)
-        out.append(f * lax.rsqrt(pivots))
+                r = row_of(s, k)
+                s = below(s, m, r, k, r * inv)
+        out += [h * lax.rsqrt(p) for h, p in zip(f, pivots)]
+        if t == 0 and fill is not None:
+            fill()
         for i in range(t + 1, len(x)):
-            p = [lane_of(x[i], at + TILE * t + k) * row_of(s, k) for k in range(TILE)]
-            while len(p) > 1:
-                p = [p[m] + p[m + 1] for m in range(0, len(p), 2)]
-            x[i] = x[i] - p[0]
+            u = [lane_of(x[i], at + TILE * t + k) for k in range(TILE)]
+            r = [row_of(s, k) for k in range(TILE)]
+            new = []
+            for h in range(2):
+                p = [u[k][h] * r[k] for k in range(TILE)]
+                while len(p) > 1:
+                    p = [p[n] + p[n + 1] for n in range(0, len(p), 2)]
+                new.append(x[i][h] - p[0])
+            x[i] = new
     return out
 
 
@@ -112,34 +135,47 @@
     a_ref[:, pl.ds(pl.multiple_of(core * HALF, HALF), HALF)] = own_ref[...]
     a_ref[:, pl.ds(pl.multiple_of((1 - core) * HALF, HALF), HALF)] = other_ref[...]
     l_ref[...] = left_ref[...]
-    sub = lax.broadcasted_iota(jnp.int32, (TILE, 128), 0)
-    lane = lax.broadcasted_iota(jnp.int32, (TILE, 128), 1)
-
-    for j in range(RANK // NB):
+    sub = lax.broadcasted_iota(jnp.int32, (8, 128), 0)
+    lane = lax.broadcasted_iota(jnp.int32, (8, 128), 1)
+
+    fill = None
+    steps = RANK // NB
+    for j in range(steps):
         j0 = j * NB
         base = j0 // 128 * 128
         at = j0 - base
         rest = 64 - at
         tiles = []
-        for i in range(NB // TILE):
-            a = a_ref[j0 + TILE * i : j0 + TILE * i + TILE, base : base + 128]
-            eye = jnp.where(lane == rest + sub + TILE * i, 1.0, 0.0)
+        for i in range(NB // 8):
+            a = a_ref[j0 + 8 * i : j0 + 8 * i + 8, base : base + 128]
+            eye = jnp.where(lane == rest + sub + 8 * i, 1.0, 0.0)
             tiles.append(jnp.where((lane >= at) & (lane < at + 64), a, eye))
-        for i, tile in enumerate(diag_inverse(tiles, at)):
-            w_ref[TILE * i : TILE * i + TILE, :] = tile
+        tiles = [tiles[i : i + 2] for i in range(0, NB // 8, 2)]
+        for i, tile in enumerate(diag_inverse(tiles, at, fill)):
+            w_ref[8 * i : 8 * i + 8, :] = tile
         w = w_ref[:, rest : rest + 64]
-        if j + 1 < RANK // NB:
-            c0 = (j0 + NB) // 128 * 128
+        panel, c0 = None, RANK
+        jn = j0 + NB
+        if j + 1 < steps:
+            c0 = jn // 128 * 128
             panel = dot(w, a_ref[j0 : j0 + NB, c0:], ((1,), (0,)), EXACT)
-            if c0 < j0 + NB:
+            if c0 < jn:
                 wide = lax.broadcasted_iota(jnp.int32, panel.shape, 1)
-                panel = jnp.where(wide >= j0 + NB - c0, panel, 0.0)
-            a_ref[c0:, c0:] -= dot(panel, panel, ((0,), (0,)), EXACT)
-        q = dot(l_ref[:, j0 : j0 + NB], w, ((1,), (1,)), EXACT)
-        q_ref[:, j0 : j0 + NB] = q.astype(bf16)
-        if j + 1 < RANK // NB:
-            l_ref[:, c0:] -= dot(q, panel, ((1,), (0,)), EXACT)
-
+                panel = jnp.where(wide >= jn - c0, panel, 0.0)
+            ahead = panel[:, jn - c0 : jn - c0 + NB]
+            a_ref[jn : jn + NB, c0:] -= dot(ahead, panel, ((0,), (0,)), EXACT)
+
+        def fill(j0=j0, w=w, panel=panel, c0=c0, jn=jn):
+            if jn + NB < RANK:
+                c1 = (jn + NB) // 128 * 128
+                below, right = panel[:, jn + NB - c0 :], panel[:, c1 - c0 :]
+                a_ref[jn + NB :, c1:] -= dot(below, right, ((0,), (0,)), EXACT)
+            q = dot(l_ref[:, j0 : j0 + NB], w, ((1,), (1,)), EXACT)
+            q_ref[:, j0 : j0 + NB] = q.astype(bf16)
+            if panel is not None:
+                l_ref[:, c0:] -= dot(q, panel, ((1,), (0,)), EXACT)
+
+    fill()
     blend_low = (mom_ref[...] + grad_ref[...].astype(f32)).astype(bf16)
     right = dot(blend_low, q_ref[...], ((1,), (0,)))
     low, high = right[:, :HALF], right[:, HALF:]
@@ -205,7 +241,10 @@
     share = enc(jnp.sum(dec(pieces, *PART), axis=0), *LEFT)
     left = dec(to_all(share, ZY, n), *LEFT).reshape(n * rows, RANK)
 
-    halves = call(gram_kernel, shape((2, 8, HALF), f32), where, left)
+    halves = call(
+        gram_kernel, shape((2, 8, HALF), f32), where, left,
+        scratch=[pltpu.VMEM((128, left.shape[0]), f32)],
+    )
     halves = jnp.broadcast_to(halves[None], (nx, 2, 8, HALF)).reshape(2 * nx, 8, HALF)
     gram_rows = jnp.sum(lax.all_to_all(halves, ("x", "core"), 0, 0), axis=0)
     gram_own = to_all(gram_rows, ZY, n).reshape(RANK, HALF)

time: 196 us -> 192 us (0.980)
  Pallas kernels: 25.9 us -> 22.5 us
    pallas_call x4, Pallas kernels: 25.9 us -> 22.5 us  [call(): pl.pallas_call(kernel, out_shape=outs, in_specs=specs, out_specs=jax.tree...]
where the time goes in v4:
time: 192 us
  blocking collectives  149 us (78%)
  Pallas kernels  22.5 us (12%)
  starting transfers between devices  10.8 us (6%)
  waiting for transfers between devices  3.85 us (2%)
  other arithmetic  2.12 us (1%)
  matrix products  2.08 us (1%)
    all_to_all x4, blocking collectives, to_all(): return lax.all_to_all(jnp.broadcast_to(x[None], (n,) + x.shape), axes, 0, 0)  74.8 us
    all_to_all x1, blocking collectives, per_device(): lax.all_to_all(enc(left_part, *PART).reshape(n, rows, RANK), ZY, 0, 0)  40.9 us
    pallas_call x4, Pallas kernels, call(): pl.pallas_call(kernel, out_shape=outs, in_specs=specs, out_specs=jax.tree...  22.5 us
    all_to_all x1, blocking collectives, per_device(): gram_rows = jnp.sum(lax.all_to_all(halves, ('x', 'core'), 0, 0), axis=0)  20.4 us
    all_to_all x1, blocking collectives, per_device(): mine = jnp.sum(dec(lax.all_to_all(part, 'x', 0, 0), *RIGHT), axis=0)  13.1 us
    ppermute x3, starting transfers between devices, swap(): return lax.ppermute(x, 'core', [(0, 1), (1, 0)])  10.8 us
    ppermute x3, waiting for transfers between devices, swap(): return lax.ppermute(x, 'core', [(0, 1), (1, 0)])  3.85 us
  transfers between devices with their start and end apart: 3, of which 3 were waited for; matrix products, arithmetic and copies ran while one was open for 0% of the time, Pallas kernels for 0%

profile of v4, /device:TPU:1, one launch (start us, length us, event | category | flops | bytes accessed | tf_op | source)
XLA Modules:
  0.0 191.6 jit_solution(14705413102894265018)
XLA Ops:
  0.6 0.1 pad_add_fusion.where_ref
  0.7 2.1 %fusion.20 = f32[512,512]{1,0:T(8,128)S(1)} fusion(f32[512,448]{0,1:T(8,128)} %param.3, bf16[512,448]{0,1:T(8,128)(2,1)} %param.4, f32[448,512]{1,0:T(8,128)} %param.5), kind=kOutput, calls=%fused_computation.35 | convolution fusion | flops 235798528 | bytes 3342336 | tf_op jit(solution)/shard_map/dot_general | solution.py:232
  2.8 0.7 fusion.14
  3.5 40.9 %all_to_all.35 = f16[64,8,512]{2,1,0:T(8,128)(2,1)S(1)} all-to-all(f16[64,8,512]{2,1,0:T(8,128)(2,1)S(1)} %fusion.14), channel_id=1, replica_groups=mesh['z'=8,'y'=8,'x'=8,'core'=2] {'z','y'}, dimensions={0} | all-to-all | bytes 1048576 | tf_op jit(solution)/shard_map/all_to_all | solution.py:240
  44.4 0.3 fusion.7
  44.7 22.5 %all_to_all.36 = f16[64,8,512]{2,1,0:T(8,128)(2,1)S(1)} all-to-all(f16[64,8,512]{2,1,0:T(8,128)(2,1)S(1)} %broadcast_in_dim.12), channel_id=1, replica_groups=mesh['z'=8,'y'=8,'x'=8,'core'=2] {'z','y'}, dimensions={0} | all-to-all | bytes 1048576 | tf_op jit(solution)/shard_map/all_to_all | solution.py:220
  67.2 0.2 fusion.10.left_ref
  67.5 1.2 shard_map.58
  68.7 20.4 %all_to_all.37 = f32[16,8,256]{2,1,0:T(8,128)S(1)} all-to-all(f32[16,8,256]{2,1,0:T(8,128)S(1)} %bitcast.30), channel_id=1, replica_groups=mesh['z'=8,'y'=8,'x'=8,'core'=2] {'x','core'}, dimensions={0} | all-to-all | bytes 262144 | tf_op jit(solution)/shard_map/all_to_all | solution.py:249
  89.1 0.0 copy-start
  89.1 0.0 copy-start.1
  89.1 22.8 %all_to_all.38 = f32[64,8,256]{2,1,0:T(8,128)S(1)} all-to-all(f32[64,8,256]{2,1,0:T(8,128)S(1)} %broadcast_in_dim.14), channel_id=1, replica_groups=mesh['z'=8,'y'=8,'x'=8,'core'=2] {'z','y'}, dimensions={0} | all-to-all | bytes 1048576 | tf_op jit(solution)/shard_map/all_to_all | solution.py:220
  111.9 3.4 %collective-permute-start = (f32[512,256]{1,0:T(8,128)S(1)}, f32[512,256]{1,0:T(8,128)S(1)}, u32[]{:S(2)}, u32[]{:S(2)}) collective-permute-start(f32[512,256]{1,0:T(8,128)S(1)} %bitcast.24), channel_id=1, source_target_pairs={{0,1},{1,0},{2,3},{3,2},{4,5},{5,4},{6,7},{7,6},{8,9},{9,8},{10,11... | collective-permute-start | bytes 1572872 | tf_op jit(solution)/shard_map/ppermute | solution.py:224
  115.3 1.3 collective-permute-done.other_ref
  116.6 0.0 copy-done
  116.6 0.0 copy-done.1
  116.6 18.6 %shard_map.59 = (bf16[512,512]{1,0:T(8,128)(2,1)S(1)}, f32[448,256]{1,0:T(8,128)S(1)}, f32[448,256]{1,0:T(8,128)S(1)}) custom-call(s32[2]{0:T(128)S(1)} %pad_add_fusion.where_ref, f32[512,256]{1,0:T(8,128)S(1)} %bitcast.25, f32[512,256]{1,0:T(8,128)S(1)} %collective-permute-done.other_ref, f32[512,512]{1,0:T(8,128)S(1)} %fusion.10.left_ref, ...), custom_call_target="tpu_custom_call" | custom-call | tf_op jit(solution)/shard_map/pallas_call | solution.py:42
  135.2 2.3 %collective-permute-start.1 = (f32[448,256]{1,0:T(8,128)S(1)}, f32[448,256]{1,0:T(8,128)S(1)}, u32[]{:S(2)}, u32[]{:S(2)}) collective-permute-start(f32[448,256]{1,0:T(8,128)S(1)} %get-tuple-element.15), channel_id=1, source_target_pairs={{0,1},{1,0},{2,3},{3,2},{4,5},{5,4},{6,7},{7,6},{8,9},{9,8},{10,11... | collective-permute-start | bytes 1376264 | tf_op jit(solution)/shard_map/ppermute | solution.py:224
  137.5 1.4 collective-permute-done.1
  138.9 0.3 fusion.16
  139.3 13.1 %all_to_all.39 = f16[8,56,256]{2,1,0:T(8,128)(2,1)S(1)} all-to-all(f16[8,56,256]{2,1,0:T(8,128)(2,1)S(1)} %bitcast.29), channel_id=1, replica_groups=mesh['z'=8,'y'=8,'x'=8,'core'=2] {'x'}, dimensions={0} | all-to-all | bytes 458752 | tf_op jit(solution)/shard_map/all_to_all | solution.py:260
  152.4 0.1 fusion.19
  152.6 11.3 %all_to_all.40 = f16[8,56,256]{2,1,0:T(8,128)(2,1)S(1)} all-to-all(f16[8,56,256]{2,1,0:T(8,128)(2,1)S(1)} %broadcast_in_dim.15), channel_id=1, replica_groups=mesh['z'=8,'y'=8,'x'=8,'core'=2] {'x'}, dimensions={0} | all-to-all | bytes 458752 | tf_op jit(solution)/shard_map/all_to_all | solution.py:220
  163.9 5.2 %collective-permute-start.2 = (f16[448,256]{1,0:T(8,128)(2,1)S(1)}, f16[448,256]{1,0:T(8,128)(2,1)S(1)}, u32[]{:S(2)}, u32[]{:S(2)}) collective-permute-start(f16[448,256]{1,0:T(8,128)(2,1)S(1)} %bitcast.28), channel_id=1, source_target_pairs={{0,1},{1,0},{2,3},{3,2},{4,5},{5,4},{6,7},{7,6},{8,9},{9,8},{10,11... | collective-permute-start | bytes 688136 | tf_op jit(solution)/shard_map/ppermute | solution.py:224
  169.1 1.1 collective-permute-done.2
  170.1 0.1 broadcast_select_fusion.1
  170.3 0.2 fusion.12.right_ref
  170.5 1.4 shard_map.60
  171.9 0.1 broadcast_in_dim.17
  172.0 18.3 %all_to_all.41 = f32[64,1,512]{2,1,0:T(1,128)S(1)} all-to-all(f32[64,1,512]{2,1,0:T(1,128)S(1)} %broadcast_in_dim.17), channel_id=1, replica_groups=mesh['z'=8,'y'=8,'x'=8,'core'=2] {'z','y'}, dimensions={0} | all-to-all | bytes 262144 | tf_op jit(solution)/shard_map/all_to_all | solution.py:220
  190.3 1.3 shard_map.61
  (8 shorter events, 0.2 us)
Async XLA Ops:
  89.1 27.6 %copy-start = (f32[512,448]{0,1:T(8,128)S(1)}, f32[512,448]{0,1:T(8,128)}, u32[]{:S(2)}) copy-start(f32[512,448]{0,1:T(8,128)} %param.3) | copy-start | bytes 2752516
  89.1 27.5 %copy-start.1 = (bf16[512,448]{0,1:T(8,128)(2,1)S(1)}, bf16[512,448]{0,1:T(8,128)(2,1)}, u32[]{:S(2)}) copy-start(bf16[512,448]{0,1:T(8,128)(2,1)} %param.4) | copy-start | bytes 1376260
  111.9 4.7 %collective-permute-start = (f32[512,256]{1,0:T(8,128)S(1)}, f32[512,256]{1,0:T(8,128)S(1)}, u32[]{:S(2)}, u32[]{:S(2)}) collective-permute-start(f32[512,256]{1,0:T(8,128)S(1)} %bitcast.24), channel_id=1, source_target_pairs={{0,1},{1,0},{2,3},{3,2},{4,5},{5,4},{6,7},{7,6},{8,9},{9,8},{10,11... | collective-permute-start | bytes 1572872 | tf_op jit(solution)/shard_map/ppermute | solution.py:224
  135.2 3.7 %collective-permute-start.1 = (f32[448,256]{1,0:T(8,128)S(1)}, f32[448,256]{1,0:T(8,128)S(1)}, u32[]{:S(2)}, u32[]{:S(2)}) collective-permute-start(f32[448,256]{1,0:T(8,128)S(1)} %get-tuple-element.15), channel_id=1, source_target_pairs={{0,1},{1,0},{2,3},{3,2},{4,5},{5,4},{6,7},{7,6},{8,9},{9,8},{10,11... | collective-permute-start | bytes 1376264 | tf_op jit(solution)/shard_map/ppermute | solution.py:224
  163.9 6.3 %collective-permute-start.2 = (f16[448,256]{1,0:T(8,128)(2,1)S(1)}, f16[448,256]{1,0:T(8,128)(2,1)S(1)}, u32[]{:S(2)}, u32[]{:S(2)}) collective-permute-start(f16[448,256]{1,0:T(8,128)(2,1)S(1)} %bitcast.28), channel_id=1, source_target_pairs={{0,1},{1,0},{2,3},{3,2},{4,5},{5,4},{6,7},{7,6},{8,9},{9,8},{10,11... | collective-permute-start | bytes 688136 | tf_op jit(solution)/shard_map/ppermute | solution.py:224

commit v5 on v4

--- a/solution.py
+++ b/solution.py
@@ -183,11 +183,9 @@
     send_ref[...] = jnp.where(core == 0, high, low)
 
 
-def momentum_kernel(right_ref, q_ref, mom_ref, grad_ref, out_ref, squares_ref):
-    right = right_ref[...]
-    feed = dot(right.astype(bf16), q_ref[...], ((1,), (1,)))
+def momentum_kernel(right_ref, q_ref, mom_ref, grad_ref, out_ref):
+    feed = dot(right_ref[...].astype(bf16), q_ref[...], ((1,), (1,)))
     out_ref[...] = mom_ref[...] + grad_ref[...].astype(f32) - feedback * feed
-    squares_ref[...] = jnp.sum(right * right, axis=0, keepdims=True)
 
 
 def update_kernel(right_ref, q_ref, squares_ref, factor_ref, update_ref):
@@ -260,16 +258,18 @@
     mine = jnp.sum(dec(lax.all_to_all(part, "x", 0, 0), *RIGHT), axis=0)
     own = to_all(enc(mine, *RIGHT), "x", nx).reshape(width, HALF)
     other = swap(own)
+
     low = jnp.where(core == 0, own, other)
     high = jnp.where(core == 0, other, own)
     right = dec(jnp.concatenate([low, high], axis=1), *RIGHT)
-
-    momentum_t, squares = call(
+    squares = jnp.sum(right * right, axis=0, keepdims=True)
+    squares = to_all(squares, ZY, n).reshape(n, RANK)
+
+    momentum_t = call(
         momentum_kernel,
-        (shape((width, left.shape[0]), f32), shape((1, RANK), f32)),
+        shape((width, left.shape[0]), f32),
         right, left_low, mom_t, grad_t,
     )
-    squares = to_all(squares, ZY, n).reshape(n, RANK)
     factor_new, update_t = call(
         update_kernel,
         (shape((width, RANK), f32), shape((width, left.shape[0]), bf16)),

time: 192 us -> 192 us (level)
  blocking collectives: 149 us -> 131 us
  waiting for transfers between devices: 3.85 us -> 14 us
  starting transfers between devices: 10.8 us -> 17.8 us
    all_to_all x4 -> x3, blocking collectives: 74.8 us -> 56.5 us  [to_all(): return lax.all_to_all(jnp.broadcast_to(x[None], (n,) + x.shape), axes, 0, 0)]
    all_to_all x0 -> x1, waiting for transfers between devices: none -> 10.2 us  [to_all(): return lax.all_to_all(jnp.broadcast_to(x[None], (n,) + x.shape), axes, 0, 0)]
    all_to_all x0 -> x1, starting transfers between devices: none -> 6.94 us  [to_all(): return lax.all_to_all(jnp.broadcast_to(x[None], (n,) + x.shape), axes, 0, 0)]
  transfers between devices with their start and end apart: 3 -> 4, of which waited for: 3 -> 4; matrix products, arithmetic and copies ran while one was open for 0% -> 0% of each run, Pallas kernels for 0% -> 1%
where the time goes in v5:
time: 192 us; the launch traced here: 191 us
  blocking collectives  131 us (68%)
  Pallas kernels  22.5 us (12%)
  starting transfers between devices  17.8 us (9%)
  waiting for transfers between devices  14 us (7%)
  other arithmetic  2.2 us (1%)
  matrix products  2.08 us (1%)
    all_to_all x3, blocking collectives, to_all(): return lax.all_to_all(jnp.broadcast_to(x[None], (n,) + x.shape), axes, 0, 0)  56.5 us
    all_to_all x1, blocking collectives, per_device(): lax.all_to_all(enc(left_part, *PART).reshape(n, rows, RANK), ZY, 0, 0)  40.9 us
    pallas_call x4, Pallas kernels, call(): pl.pallas_call(kernel, out_shape=outs, in_specs=specs, out_specs=jax.tree...  22.5 us
    all_to_all x1, blocking collectives, per_device(): gram_rows = jnp.sum(lax.all_to_all(halves, ('x', 'core'), 0, 0), axis=0)  20.4 us
    all_to_all x1, blocking collectives, per_device(): mine = jnp.sum(dec(lax.all_to_all(part, 'x', 0, 0), *RIGHT), axis=0)  13.1 us
    ppermute x3, starting transfers between devices, swap(): return lax.ppermute(x, 'core', [(0, 1), (1, 0)])  10.8 us
    all_to_all x1, waiting for transfers between devices, to_all(): return lax.all_to_all(jnp.broadcast_to(x[None], (n,) + x.shape), axes, 0, 0)  10.2 us
    all_to_all x1, starting transfers between devices, to_all(): return lax.all_to_all(jnp.broadcast_to(x[None], (n,) + x.shape), axes, 0, 0)  6.94 us
  transfers between devices with their start and end apart: 4, of which 4 were waited for; matrix products, arithmetic and copies ran while one was open for 0% of the time, Pallas kernels for 1%

profile of v5, /device:TPU:1, one launch (start us, length us, event | category | flops | bytes accessed | tf_op | source)
XLA Modules:
  0.0 191.1 jit_solution(16397077465388288438)
XLA Ops:
  0.6 0.1 pad_add_fusion.where_ref
  0.7 2.1 %fusion.20 = f32[512,512]{1,0:T(8,128)S(1)} fusion(f32[512,448]{0,1:T(8,128)} %param.3, bf16[512,448]{0,1:T(8,128)(2,1)} %param.4, f32[448,512]{1,0:T(8,128)} %param.5), kind=kOutput, calls=%fused_computation.36 | convolution fusion | flops 235798528 | bytes 3342336 | tf_op jit(solution)/shard_map/dot_general | solution.py:230
  2.8 0.7 fusion.14
  3.5 40.9 %all_to_all.35 = f16[64,8,512]{2,1,0:T(8,128)(2,1)S(1)} all-to-all(f16[64,8,512]{2,1,0:T(8,128)(2,1)S(1)} %fusion.14), channel_id=1, replica_groups=mesh['z'=8,'y'=8,'x'=8,'core'=2] {'z','y'}, dimensions={0} | all-to-all | bytes 1048576 | tf_op jit(solution)/shard_map/all_to_all | solution.py:238
  44.4 0.3 fusion.7
  44.7 22.5 %all_to_all.36 = f16[64,8,512]{2,1,0:T(8,128)(2,1)S(1)} all-to-all(f16[64,8,512]{2,1,0:T(8,128)(2,1)S(1)} %broadcast_in_dim.10), channel_id=1, replica_groups=mesh['z'=8,'y'=8,'x'=8,'core'=2] {'z','y'}, dimensions={0} | all-to-all | bytes 1048576 | tf_op jit(solution)/shard_map/all_to_all | solution.py:218
  67.2 0.2 fusion.10.left_ref
  67.5 1.2 shard_map.58
  68.7 20.4 %all_to_all.37 = f32[16,8,256]{2,1,0:T(8,128)S(1)} all-to-all(f32[16,8,256]{2,1,0:T(8,128)S(1)} %bitcast.29), channel_id=1, replica_groups=mesh['z'=8,'y'=8,'x'=8,'core'=2] {'x','core'}, dimensions={0} | all-to-all | bytes 262144 | tf_op jit(solution)/shard_map/all_to_all | solution.py:247
  89.1 0.0 copy-start
  89.1 0.0 copy-start.1
  89.1 22.8 %all_to_all.38 = f32[64,8,256]{2,1,0:T(8,128)S(1)} all-to-all(f32[64,8,256]{2,1,0:T(8,128)S(1)} %broadcast_in_dim.12), channel_id=1, replica_groups=mesh['z'=8,'y'=8,'x'=8,'core'=2] {'z','y'}, dimensions={0} | all-to-all | bytes 1048576 | tf_op jit(solution)/shard_map/all_to_all | solution.py:218
  111.9 3.4 %collective-permute-start = (f32[512,256]{1,0:T(8,128)S(1)}, f32[512,256]{1,0:T(8,128)S(1)}, u32[]{:S(2)}, u32[]{:S(2)}) collective-permute-start(f32[512,256]{1,0:T(8,128)S(1)} %bitcast.23), channel_id=1, source_target_pairs={{0,1},{1,0},{2,3},{3,2},{4,5},{5,4},{6,7},{7,6},{8,9},{9,8},{10,11... | collective-permute-start | bytes 1572872 | tf_op jit(solution)/shard_map/ppermute | solution.py:222
  115.3 1.3 collective-permute-done.other_ref
  116.6 0.0 copy-done
  116.6 0.0 copy-done.1
  116.6 18.6 %shard_map.59 = (bf16[512,512]{1,0:T(8,128)(2,1)S(1)}, f32[448,256]{1,0:T(8,128)S(1)}, f32[448,256]{1,0:T(8,128)S(1)}) custom-call(s32[2]{0:T(128)S(1)} %pad_add_fusion.where_ref, f32[512,256]{1,0:T(8,128)S(1)} %bitcast.24, f32[512,256]{1,0:T(8,128)S(1)} %collective-permute-done.other_ref, f32[512,512]{1,0:T(8,128)S(1)} %fusion.10.left_ref, ...), custom_call_target="tpu_custom_call" | custom-call | tf_op jit(solution)/shard_map/pallas_call | solution.py:42
  135.2 2.3 %collective-permute-start.1 = (f32[448,256]{1,0:T(8,128)S(1)}, f32[448,256]{1,0:T(8,128)S(1)}, u32[]{:S(2)}, u32[]{:S(2)}) collective-permute-start(f32[448,256]{1,0:T(8,128)S(1)} %get-tuple-element.13), channel_id=1, source_target_pairs={{0,1},{1,0},{2,3},{3,2},{4,5},{5,4},{6,7},{7,6},{8,9},{9,8},{10,11... | collective-permute-start | bytes 1376264 | tf_op jit(solution)/shard_map/ppermute | solution.py:222
  137.5 1.4 collective-permute-done.1
  138.9 0.3 fusion.16
  139.3 13.1 %all_to_all.39 = f16[8,56,256]{2,1,0:T(8,128)(2,1)S(1)} all-to-all(f16[8,56,256]{2,1,0:T(8,128)(2,1)S(1)} %bitcast.28), channel_id=1, replica_groups=mesh['z'=8,'y'=8,'x'=8,'core'=2] {'x'}, dimensions={0} | all-to-all | bytes 458752 | tf_op jit(solution)/shard_map/all_to_all | solution.py:258
  152.4 0.1 fusion.19
  152.6 11.3 %all_to_all.40 = f16[8,56,256]{2,1,0:T(8,128)(2,1)S(1)} all-to-all(f16[8,56,256]{2,1,0:T(8,128)(2,1)S(1)} %broadcast_in_dim.13), channel_id=1, replica_groups=mesh['z'=8,'y'=8,'x'=8,'core'=2] {'x'}, dimensions={0} | all-to-all | bytes 458752 | tf_op jit(solution)/shard_map/all_to_all | solution.py:218
  163.9 5.2 %collective-permute-start.2 = (f16[448,256]{1,0:T(8,128)(2,1)S(1)}, f16[448,256]{1,0:T(8,128)(2,1)S(1)}, u32[]{:S(2)}, u32[]{:S(2)}) collective-permute-start(f16[448,256]{1,0:T(8,128)(2,1)S(1)} %bitcast.27), channel_id=1, source_target_pairs={{0,1},{1,0},{2,3},{3,2},{4,5},{5,4},{6,7},{7,6},{8,9},{9,8},{10,11... | collective-permute-start | bytes 688136 | tf_op jit(solution)/shard_map/ppermute | solution.py:222
  169.1 1.1 collective-permute-done.2
  170.1 0.1 broadcast_select_fusion.1
  170.3 0.3 multiply_reduce_fusion
  170.6 0.7 broadcast_in_dim.14
  171.3 6.9 %all-to-all-start.6 = ((f32[64,1,512]{2,1,0:T(1,128)}), f32[64,1,512]{2,1,0:T(1,128)S(1)}, u32[]{:S(2)}, u32[]{:S(2)}) async-start(f32[64,1,512]{2,1,0:T(1,128)} %broadcast_in_dim.14), calls=%async_computation.6 | async-start | bytes 262144 | tf_op jit(solution)/shard_map/all_to_all | solution.py:218
  178.3 1.4 shard_map.60
  179.6 10.2 %all-to-all-done.6 = f32[64,1,512]{2,1,0:T(1,128)S(1)} async-done(((f32[64,1,512]{2,1,0:T(1,128)}), f32[64,1,512]{2,1,0:T(1,128)S(1)}, u32[]{:S(2)}, u32[]{:S(2)}) %all-to-all-start.6) | async-done | bytes 131104 | tf_op jit(solution)/shard_map/all_to_all | solution.py:218
  189.8 1.3 shard_map.61
  (8 shorter events, 0.2 us)
Async XLA Ops:
  89.1 27.6 %copy-start = (f32[512,448]{0,1:T(8,128)S(1)}, f32[512,448]{0,1:T(8,128)}, u32[]{:S(2)}) copy-start(f32[512,448]{0,1:T(8,128)} %param.3) | copy-start | bytes 2752516
  89.1 27.5 %copy-start.1 = (bf16[512,448]{0,1:T(8,128)(2,1)S(1)}, bf16[512,448]{0,1:T(8,128)(2,1)}, u32[]{:S(2)}) copy-start(bf16[512,448]{0,1:T(8,128)(2,1)} %param.4) | copy-start | bytes 1376260
  111.9 4.7 %collective-permute-start = (f32[512,256]{1,0:T(8,128)S(1)}, f32[512,256]{1,0:T(8,128)S(1)}, u32[]{:S(2)}, u32[]{:S(2)}) collective-permute-start(f32[512,256]{1,0:T(8,128)S(1)} %bitcast.23), channel_id=1, source_target_pairs={{0,1},{1,0},{2,3},{3,2},{4,5},{5,4},{6,7},{7,6},{8,9},{9,8},{10,11... | collective-permute-start | bytes 1572872 | tf_op jit(solution)/shard_map/ppermute | solution.py:222
  135.2 3.7 %collective-permute-start.1 = (f32[448,256]{1,0:T(8,128)S(1)}, f32[448,256]{1,0:T(8,128)S(1)}, u32[]{:S(2)}, u32[]{:S(2)}) collective-permute-start(f32[448,256]{1,0:T(8,128)S(1)} %get-tuple-element.13), channel_id=1, source_target_pairs={{0,1},{1,0},{2,3},{3,2},{4,5},{5,4},{6,7},{7,6},{8,9},{9,8},{10,11... | collective-permute-start | bytes 1376264 | tf_op jit(solution)/shard_map/ppermute | solution.py:222
  163.9 6.3 %collective-permute-start.2 = (f16[448,256]{1,0:T(8,128)(2,1)S(1)}, f16[448,256]{1,0:T(8,128)(2,1)S(1)}, u32[]{:S(2)}, u32[]{:S(2)}) collective-permute-start(f16[448,256]{1,0:T(8,128)(2,1)S(1)} %bitcast.27), channel_id=1, source_target_pairs={{0,1},{1,0},{2,3},{3,2},{4,5},{5,4},{6,7},{7,6},{8,9},{9,8},{10,11... | collective-permute-start | bytes 688136 | tf_op jit(solution)/shard_map/ppermute | solution.py:222
  171.3 18.5 %all-to-all-start.6 = ((f32[64,1,512]{2,1,0:T(1,128)}), f32[64,1,512]{2,1,0:T(1,128)S(1)}, u32[]{:S(2)}, u32[]{:S(2)}) async-start(f32[64,1,512]{2,1,0:T(1,128)} %broadcast_in_dim.14), calls=%async_computation.6 | async-start | bytes 262144 | tf_op jit(solution)/shard_map/all_to_all | solution.py:218
